TPU v7x, 32 devices: a whole 2x2x4 slice. The times are simulated.
32 devices in a mesh: groups: 2 (over x), gx: 8 (over z, y), gy: 2 (over core).
Axes of the slice: x: 2, y: 2, z: 4, core: 2. Of those that a mesh axis runs over, the one named last changes fastest.
Arguments:
- inputs: bfloat16 [1024, 8192], P(('groups', 'gx'), 'gy'), parts along dimension 0, may hold values from -6 to 6
- out_grad: bfloat16 [1024, 8192], P(('groups', 'gx'), 'gy'), parts along dimension 0, may hold values from -1.5 to 1.5
- w_gate: bfloat16 [8192, 14336], P('gy', 'gx'), may hold values from -0.0625 to 0.0625
- w_up: bfloat16 [8192, 14336], P('gy', 'gx'), may hold values from -0.0625 to 0.0625
- w_down: bfloat16 [14336, 8192], P('gx', 'gy'), may hold values from -0.046875 to 0.046875
Outputs:
- input_grad: bfloat16 [1024, 8192], P(('groups', 'gx'), 'gy'), parts along dimension 0
- gate_wgrad: bfloat16 [16384, 14336], P(('groups', 'gy'), 'gx'), parts along dimension 0
- up_wgrad: bfloat16 [16384, 14336], P(('groups', 'gy'), 'gx'), parts along dimension 0
- down_wgrad: bfloat16 [28672, 8192], P(('groups', 'gx'), 'gy'), parts along dimension 0
There are 2 independent parts, one for each index of `groups`. A program takes and returns all parts, laid end to end along the dimension named above; an argument that names none is the same for every part. Nothing has to cross between parts.
All inputs are finite; a program needn't handle non-finite values.
Results may differ from a plain program's by a relative error of at most 0.005.
Values may be sent and summed in bfloat16 or wider, within the bound.
No kernel may reach another device: no remote copies, remote signals or barrier semaphores. Data moves between devices by JAX's collectives and lax.ppermute only.
A program may use at most 256 MiB of HBM per device.

v0:
```python
import jax
import jax.numpy as jnp
from jax import lax
from jax.sharding import PartitionSpec as P


def swiglu_back(gate_pre, up_pre, hidden_grad):
    sig = jax.nn.sigmoid(gate_pre)
    silu_val = gate_pre * sig
    hidden = (silu_val * up_pre).astype(jnp.bfloat16)
    gate_back = (hidden_grad * up_pre * sig * (1.0 + gate_pre * (1.0 - sig))).astype(jnp.bfloat16)
    up_back = (hidden_grad * silu_val).astype(jnp.bfloat16)
    return (hidden, gate_back, up_back)


def body(inputs, out_grad, w_gate, w_up, w_down):
    gathered_in, gathered_grad = (
        lax.all_gather(inputs, "gx", axis=0, tiled=True),
        lax.all_gather(out_grad, "gx", axis=0, tiled=True),
    )
    gate_part = jnp.dot(gathered_in, w_gate, preferred_element_type=jnp.float32)
    up_part = jnp.dot(gathered_in, w_up, preferred_element_type=jnp.float32)
    back_part = lax.dot_general(
        gathered_grad, w_down, (((1,), (1,)), ((), ())), preferred_element_type=jnp.float32
    )
    gate_pre, up_pre, hidden_grad = lax.psum((gate_part, up_part, back_part), "gy")
    hidden, gate_back, up_back = swiglu_back(gate_pre, up_pre, hidden_grad)
    contract_rows = (((0,), (0,)), ((), ()))
    down_wgrad = lax.dot_general(
        hidden, gathered_grad, contract_rows, preferred_element_type=jnp.float32
    ).astype(jnp.bfloat16)
    gate_wgrad = lax.dot_general(
        gathered_in, gate_back, contract_rows, preferred_element_type=jnp.float32
    ).astype(jnp.bfloat16)
    up_wgrad = lax.dot_general(
        gathered_in, up_back, contract_rows, preferred_element_type=jnp.float32
    ).astype(jnp.bfloat16)
    contract_last = (((1,), (1,)), ((), ()))
    result = lax.dot_general(gate_back, w_gate, contract_last, preferred_element_type=jnp.float32)
    summed = lax.psum_scatter(
        result + lax.dot_general(up_back, w_up, contract_last, preferred_element_type=jnp.float32),
        "gx",
        scatter_dimension=0,
        tiled=True,
    )
    input_grad = summed.astype(jnp.bfloat16)
    return (input_grad, gate_wgrad, up_wgrad, down_wgrad)


def solution(mesh):
    in_specs = (
        P(("groups", "gx"), "gy"),
        P(("groups", "gx"), "gy"),
        P("gy", "gx"),
        P("gy", "gx"),
        P("gx", "gy"),
    )
    out_specs = (
        P(("groups", "gx"), "gy"),
        P(("groups", "gy"), "gx"),
        P(("groups", "gy"), "gx"),
        P(("groups", "gx"), "gy"),
    )
    return jax.shard_map(body, mesh=mesh, in_specs=in_specs, out_specs=out_specs, check_vma=False)
```

profile of v0, /device:TPU:0, one launch (start us, length us, event | category | flops | bytes accessed | tf_op | source)
XLA Modules:
  0.0 421.3 jit_solution(16129677953749112571)
XLA Ops:
  7.2 0.0 all-gather.5.cloned.1.call-start
  7.2 0.7 all-gather.5.cloned.1.call-update
  7.9 0.0 all-gather.3.cloned.1.call-start
  7.9 0.7 all-gather.3.cloned.1.call-update
  8.6 0.0 all-reduce.3.cloned.1.call-start
  8.7 77.6 %all-gather.5.cloned.1.call-done = bf16[512,4096]{1,0:T(8,128)(2,1)} async-done(((bf16[64,4096]{1,0:T(8,128)(2,1)}), bf16[512,4096]{1,0:T(8,128)(2,1)}) %all-gather.5.cloned.1.call-update) | async-done | bytes 4194320 | tf_op jit(solution)/shard_map/all_gather | solution.py:18
  86.3 0.0 copy-start.1
  86.3 16.6 %fusion.7 = f32[512,1792]{1,0:T(8,128)} fusion(bf16[512,4096]{1,0:T(8,128)(2,1)} %all-gather.5.cloned.1.call-done, bf16[4096,1792]{1,0:T(8,128)(2,1)} %param.7), kind=kOutput, calls=%fused_computation.14 | convolution fusion | flops 7516192768 | bytes 22544384 | tf_op jit(solution)/shard_map/dot_general | solution.py:21
  102.9 0.0 copy-done.1
  102.9 12.9 %fusion.6 = f32[512,1792]{1,0:T(8,128)} fusion(bf16[512,4096]{1,0:T(8,128)(2,1)S(1)} %copy-done.1, bf16[4096,1792]{1,0:T(8,128)(2,1)} %param.8), kind=kOutput, calls=%fused_computation.13 | convolution fusion | flops 7516192768 | bytes 22544384 | tf_op jit(solution)/shard_map/dot_general | solution.py:22
  115.8 44.3 %all-gather.3.cloned.1.call-done = bf16[512,4096]{1,0:T(8,128)(2,1)} async-done(((bf16[64,4096]{1,0:T(8,128)(2,1)}), bf16[512,4096]{1,0:T(8,128)(2,1)}) %all-gather.3.cloned.1.call-update) | async-done | bytes 4194320 | tf_op jit(solution)/shard_map/all_gather | solution.py:19
  160.1 14.6 %fusion.5 = f32[512,1792]{1,0:T(8,128)} fusion(bf16[512,4096]{1,0:T(8,128)(2,1)} %all-gather.3.cloned.1.call-done, bf16[1792,4096]{1,0:T(8,128)(2,1)} %param.9), kind=kOutput, calls=%fused_computation.12 | convolution fusion | flops 7516192768 | bytes 22544384 | tf_op jit(solution)/shard_map/dot_general | solution.py:23
  174.6 0.0 all-reduce.3.cloned.1.call-update
  174.7 0.2 reduce-scatter.2.cloned.1.call-start
  174.9 42.1 %all-reduce.3.cloned.1.call-done = (f32[512,1792]{1,0:T(8,128)}, f32[512,1792]{1,0:T(8,128)}, f32[512,1792]{1,0:T(8,128)}) async-done(((f32[512,1792]{1,0:T(8,128)}, f32[512,1792]{1,0:T(8,128)}, f32[512,1792]{1,0:T(8,128)}), (f32[512,1792]{1,0:T(8,128)}, f32[512,1792]{1,0:T(8,128)}, f32[512,1792]{1,0:T(8,128)})) %all-reduce.3.cloned.1.call-update) | async-done | bytes 11010064 | tf_op jit(solution)/shard_map/psum | solution.py:26
  217.0 5.1 %multiply_convert_fusion.1 = (bf16[512,1792]{1,0:T(8,128)(2,1)S(1)}, bf16[512,1792]{1,0:T(8,128)(2,1)S(1)}) fusion(f32[512,1792]{1,0:T(8,128)} %get-tuple-element.9, f32[512,1792]{1,0:T(8,128)} %get-tuple-element.8, f32[512,1792]{1,0:T(8,128)} %get-tuple-element.10), kind=kLoop, calls=%fused_computation.7 | loop fusion | flops 11927552 | bytes 14680064 | tf_op jit(solution)/shard_map/convert_element_type | solution.py:12
  222.1 0.0 copy-start
  222.1 13.7 %fusion.8 = f32[512,4096]{1,0:T(8,128)} fusion(bf16[512,1792]{1,0:T(8,128)(2,1)S(1)} %get-tuple-element.12, bf16[4096,1792]{1,0:T(8,128)(2,1)} %param.7), kind=kOutput, calls=%fused_computation.15 | convolution fusion | flops 7516192768 | bytes 24903680 | tf_op jit(solution)/shard_map/dot_general | solution.py:39
  235.9 0.0 copy-done
  235.9 26.5 %convolution_add_fusion = f32[512,4096]{1,0:T(8,128)} fusion(f32[512,4096]{1,0:T(8,128)} %fusion.8, bf16[512,1792]{1,0:T(8,128)(2,1)S(1)} %get-tuple-element.11, bf16[4096,1792]{1,0:T(8,128)(2,1)} %param.8), kind=kOutput, calls=%fused_computation.5 | convolution fusion | flops 7518289920 | bytes 33292288 | tf_op jit(solution)/shard_map/dot_general | solution.py:41
  262.3 0.0 reduce-scatter.2.cloned.1.call-update
  262.4 13.6 %fusion = bf16[4096,1792]{0,1:T(8,128)(2,1)} fusion(bf16[512,1792]{1,0:T(8,128)(2,1)} %copy-done, bf16[512,4096]{1,0:T(8,128)(2,1)} %all-gather.5.cloned.1.call-done), kind=kOutput, calls=%fused_computation.3 | convolution fusion | flops 7523532800 | bytes 20709376 | tf_op jit(solution)/shard_map/dot_general | solution.py:32
  275.9 18.7 %copy.9 = bf16[4096,1792]{1,0:T(8,128)(2,1)} copy(bf16[4096,1792]{0,1:T(8,128)(2,1)} %fusion) | data formatting | bytes 29360128
  294.7 13.4 %fusion.1 = bf16[4096,1792]{0,1:T(8,128)(2,1)} fusion(bf16[512,1792]{1,0:T(8,128)(2,1)S(1)} %get-tuple-element.11, bf16[512,4096]{1,0:T(8,128)(2,1)} %all-gather.5.cloned.1.call-done), kind=kOutput, calls=%fused_computation.4 | convolution fusion | flops 7523532800 | bytes 20709376 | tf_op jit(solution)/shard_map/dot_general | solution.py:35
  308.0 18.7 %copy.10 = bf16[4096,1792]{1,0:T(8,128)(2,1)} copy(bf16[4096,1792]{0,1:T(8,128)(2,1)} %fusion.1) | data formatting | bytes 29360128
  326.7 14.6 %convolution_convert_fusion = bf16[1792,4096]{1,0:T(8,128)(2,1)} fusion(bf16[512,4096]{1,0:T(8,128)(2,1)} %all-gather.3.cloned.1.call-done, f32[512,1792]{1,0:T(8,128)} %get-tuple-element.10, f32[512,1792]{1,0:T(8,128)} %get-tuple-element.8), kind=kOutput, calls=%fused_computation | convolution fusion | flops 7529037824 | bytes 26214400 | tf_op jit(solution)/shard_map/dot_general | solution.py:29
  341.3 71.3 %reduce-scatter.2.cloned.1.call-done = f32[64,4096]{1,0:T(8,128)} async-done(((f32[512,4096]{1,0:T(8,128)}), f32[64,4096]{1,0:T(8,128)}) %reduce-scatter.2.cloned.1.call-update) | async-done | bytes 1048592 | tf_op jit(solution)/shard_map/reduce_scatter | solution.py:40
  412.7 2.1 convert_element_type.29
Async XLA Ops:
  7.2 79.1 %all-gather.5.cloned.1.call-start = ((), (), s32[]{:S(2)}) async-start(), calls=%async_computation.2 | async-start | bytes 4718592 | tf_op jit(solution)/shard_map/all_gather | solution.py:18
  7.9 152.2 %all-gather.3.cloned.1.call-start = ((), (), s32[]{:S(2)}) async-start(), calls=%async_computation.1 | async-start | bytes 4718592 | tf_op jit(solution)/shard_map/all_gather | solution.py:19
  8.6 208.3 %all-reduce.3.cloned.1.call-start = ((), (), s32[]{:S(2)}) async-start(), calls=%async_computation.4 | async-start | bytes 22020096 | tf_op jit(solution)/shard_map/psum | solution.py:26
  86.3 16.6 %copy-start.1 = (bf16[512,4096]{1,0:T(8,128)(2,1)S(1)}, bf16[512,4096]{1,0:T(8,128)(2,1)}, u32[]{:S(2)}) copy-start(bf16[512,4096]{1,0:T(8,128)(2,1)} %all-gather.5.cloned.1.call-done) | copy-start | bytes 12582916
  174.7 238.0 %reduce-scatter.2.cloned.1.call-start = ((), (), s32[]{:S(2)}) async-start(), calls=%async_computation.3 | async-start | bytes 9437184 | tf_op jit(solution)/shard_map/reduce_scatter | solution.py:40
  222.1 13.8 %copy-start = (bf16[512,1792]{1,0:T(8,128)(2,1)}, bf16[512,1792]{1,0:T(8,128)(2,1)S(1)}, u32[]{:S(2)}) copy-start(bf16[512,1792]{1,0:T(8,128)(2,1)S(1)} %get-tuple-element.12) | copy-start | bytes 5505028
Sparse Core Ops, SparseCore 0:
  10.1 76.0 all-gather.4
  88.4 71.6 all-gather.2
  174.8 42.1 all-reduce.2
  262.5 150.1 reduce-scatter.1
where the time goes:
time: 422 us; the launch traced here: 421 us
  waiting for transfers between devices  237 us (56%)
  matrix products  126 us (30%)
  local copies, waits for them, and re-layouts  37.4 us (9%)
  between operations  13.8 us (3%)
  other arithmetic  7.17 us (2%)
    all_gather x1, waiting for transfers between devices, body(): lax.all_gather(inputs, 'gx', axis=0, tiled=True)  77.6 us
    reduce_scatter x1, waiting for transfers between devices, body(): lax.psum_scatter(result + lax.dot_general(up_back, w_up, contract_last, p...  71.3 us
    all_gather x1, waiting for transfers between devices, body(): lax.all_gather(out_grad, 'gx', axis=0, tiled=True)  44.3 us
    psum x1, waiting for transfers between devices, body(): lax.psum((gate_part, up_part, back_part), 'gy')  42.1 us
    unnamed x6, local copies, waits for them, and re-layouts  37.4 us
    dot_general x1, matrix products, body(): lax.dot_general(up_back, w_up, contract_last, preferred_element_type=jnp....  26.5 us
    dot_general x1, matrix products, body(): gate_part = jnp.dot(gathered_in, w_gate, preferred_element_type=jnp.float32)  16.6 us
    dot_general x1, matrix products, body(): lax.dot_general(hidden, gathered_grad, contract_rows, preferred_element_t...  14.6 us
  transfers between devices with their start and end apart: 4, of which 4 were waited for; matrix products, arithmetic and copies ran while one was open for 26% of the time, Pallas kernels for 0%

commit v1 on v0

v1 whole, which is shorter than its diff:
```python
import jax
import jax.numpy as jnp
from jax import lax
from jax.experimental import pallas as pl
from jax.experimental.pallas import tpu as pltpu
from jax.sharding import PartitionSpec as P

BF = jnp.bfloat16
F32 = jnp.float32
VMEM_LIMIT = 58 * 2**20
NN = (((1,), (0,)), ((), ()))
NT = (((1,), (1,)), ((), ()))
TN = (((0,), (0,)), ((), ()))


def dot(a, b, dims):
    return lax.dot_general(a, b, dims, preferred_element_type=F32)


def tile_of(extent, wanted):
    for tile in range(wanted, 127, -128):
        if extent % tile == 0:
            return tile
    return extent


def call(kernel, name, flops, nbytes, **kwargs):
    return pl.pallas_call(
        kernel,
        name=name,
        compiler_params=pltpu.CompilerParams(vmem_limit_bytes=VMEM_LIMIT),
        cost_estimate=pl.CostEstimate(flops=flops, bytes_accessed=nbytes, transcendentals=0),
        **kwargs,
    )


def gather_matmul(pieces, weight, dims, name):
    rows, depth = pieces[0].shape
    count = len(pieces)
    tokens = rows * count
    width = weight.shape[1] if dims == NN else weight.shape[0]
    tile = tile_of(width, 256)

    def kernel(*refs):
        piece_refs = refs[:count]
        w_ref, x_ref, own_ref, send_ref, sems = refs[count:]

        @pl.when(pl.program_id(0) == 0)
        def _():
            copies = [
                pltpu.make_async_copy(p, x_ref.at[pl.ds(i * rows, rows)], sems.at[i])
                for i, p in enumerate(piece_refs)
            ]
            for c in copies:
                c.start()
            for c in copies:
                c.wait()

        out = dot(x_ref[...], w_ref[...], dims)
        own_ref[...] = out
        send_ref[...] = out.astype(BF)

    w_spec = (
        pl.BlockSpec((depth, tile), lambda j: (0, j))
        if dims == NN
        else pl.BlockSpec((tile, depth), lambda j: (j, 0))
    )
    return call(
        kernel,
        name,
        2 * tokens * depth * width,
        2 * depth * width,
        grid=(width // tile,),
        in_specs=[pl.BlockSpec(memory_space=pl.ANY)] * count + [w_spec],
        out_specs=[
            pl.BlockSpec((tokens, depth), lambda j: (0, 0)),
            pl.BlockSpec((tokens, tile), lambda j: (0, j)),
            pl.BlockSpec((tokens, tile), lambda j: (0, j)),
        ],
        out_shape=[
            jax.ShapeDtypeStruct((tokens, depth), BF),
            jax.ShapeDtypeStruct((tokens, width), F32),
            jax.ShapeDtypeStruct((tokens, width), BF),
        ],
        scratch_shapes=[pltpu.SemaphoreType.DMA((count,))],
    )(*pieces, weight)


def matmul(x, weight, name):
    tokens, depth = x.shape
    width = weight.shape[1]
    tile = tile_of(width, 256)

    def kernel(x_ref, w_ref, own_ref, send_ref):
        out = dot(x_ref[...], w_ref[...], NN)
        own_ref[...] = out
        send_ref[...] = out.astype(BF)

    return call(
        kernel,
        name,
        2 * tokens * depth * width,
        2 * depth * width,
        grid=(width // tile,),
        in_specs=[
            pl.BlockSpec((tokens, depth), lambda j: (0, 0)),
            pl.BlockSpec((depth, tile), lambda j: (0, j)),
        ],
        out_specs=[pl.BlockSpec((tokens, tile), lambda j: (0, j))] * 2,
        out_shape=[
            jax.ShapeDtypeStruct((tokens, width), F32),
            jax.ShapeDtypeStruct((tokens, width), BF),
        ],
    )(x, weight)


def backward(pre, w_gate, w_up, chunk, chunks, rows, name):
    tokens, width = pre[0].shape
    depth = w_gate.shape[0]
    part = tokens // chunks
    blocks = part // rows
    tile = tile_of(depth, 512)

    def kernel(*refs):
        g_own, g_recv, u_own, u_recv, h_own, h_recv, wg_ref, wu_ref = refs[:8]
        block_refs = refs[8 : 8 + blocks]
        hidden_ref, gb_ref, ub_ref = refs[8 + blocks :]

        @pl.when(pl.program_id(0) == 0)
        def _():
            step = tile_of(width, 256)

            @pl.loop(0, width // step)
            def _(i):
                at = (slice(None), pl.ds(pl.multiple_of(i * step, step), step))
                gate_pre = g_own[at] + g_recv[at].astype(F32)
                up_pre = u_own[at] + u_recv[at].astype(F32)
                hidden_grad = h_own[at] + h_recv[at].astype(F32)
                sig = jax.nn.sigmoid(gate_pre)
                silu_val = gate_pre * sig
                hidden_ref[at] = (silu_val * up_pre).astype(BF)
                gb_ref[at] = (hidden_grad * up_pre * sig * (1.0 + gate_pre * (1.0 - sig))).astype(BF)
                ub_ref[at] = (hidden_grad * silu_val).astype(BF)

        out = dot(gb_ref[...], wg_ref[...], NT) + dot(ub_ref[...], wu_ref[...], NT)
        for i, ref in enumerate(block_refs):
            ref[...] = out[i * rows : (i + 1) * rows].astype(BF)

    whole = pl.BlockSpec((part, width), lambda j: (chunk, 0))
    return call(
        kernel,
        name,
        4 * part * depth * width,
        4 * depth * width,
        grid=(depth // tile,),
        in_specs=[whole] * 6 + [pl.BlockSpec((tile, width), lambda j: (j, 0))] * 2,
        out_specs=[pl.BlockSpec((rows, tile), lambda j: (0, j))] * blocks
        + [pl.BlockSpec((part, width), lambda j: (0, 0))] * 3,
        out_shape=[jax.ShapeDtypeStruct((rows, depth), BF)] * blocks
        + [jax.ShapeDtypeStruct((part, width), BF)] * 3,
    )(*pre, w_gate, w_up)


def weight_grads(x, chunks_of, name):
    tokens, depth = x.shape
    count = len(chunks_of)
    pieces = len(chunks_of[0])
    part, width = chunks_of[0][0].shape
    tile = tile_of(depth, 512)

    def kernel(*refs):
        x_ref = refs[0]
        y_refs = refs[1 : 1 + count * pieces]
        out_refs = refs[1 + count * pieces : 1 + count * pieces + count]
        ys = refs[1 + count * pieces + count : -1]
        sems = refs[-1]

        @pl.when(pl.program_id(0) == 0)
        def _():
            copies = [
                pltpu.make_async_copy(
                    y_refs[k * pieces + i], ys[k].at[pl.ds(i * part, part)], sems.at[k * pieces + i]
                )
                for k in range(count)
                for i in range(pieces)
            ]
            for c in copies:
                c.start()
            for c in copies:
                c.wait()

        for y, out_ref in zip(ys, out_refs):
            out_ref[...] = dot(x_ref[...], y[...], TN).astype(BF)

    return call(
        kernel,
        name,
        2 * tokens * depth * width * count,
        2 * depth * width * count,
        grid=(depth // tile,),
        in_specs=[pl.BlockSpec((tokens, tile), lambda j: (0, j))]
        + [pl.BlockSpec(memory_space=pl.ANY)] * (count * pieces),
        out_specs=[pl.BlockSpec((tile, width), lambda j: (j, 0))] * count,
        out_shape=[jax.ShapeDtypeStruct((depth, width), BF)] * count,
        scratch_shapes=[pltpu.VMEM((tokens, width), BF)] * count
        + [pltpu.SemaphoreType.DMA((count * pieces,))],
    )(x, *[y for ys in chunks_of for y in ys])


def down_grads(hidden_chunks, grad, name):
    tokens, depth = grad.shape
    pieces = len(hidden_chunks)
    part, width = hidden_chunks[0].shape
    tile = tile_of(width, 256)

    def kernel(*refs):
        h_refs, g_ref, out_ref = refs[:pieces], refs[pieces], refs[pieces + 1]
        hidden = jnp.concatenate([h[...] for h in h_refs], axis=0)
        out_ref[...] = dot(hidden, g_ref[...], TN).astype(BF)

    return call(
        kernel,
        name,
        2 * tokens * depth * width,
        2 * depth * width,
        grid=(width // tile,),
        in_specs=[pl.BlockSpec((part, tile), lambda j: (0, j))] * pieces
        + [pl.BlockSpec((tokens, depth), lambda j: (0, 0))],
        out_specs=pl.BlockSpec((tile, depth), lambda j: (j, 0)),
        out_shape=jax.ShapeDtypeStruct((width, depth), BF),
    )(*hidden_chunks, grad)


def ring_body(n, inputs, out_grad, w_gate, w_up, w_down):
    ring = n // 2
    along = [(2 * p + s, 2 * ((p + 1) % ring) + s) for p in range(ring) for s in range(2)]
    across = [(i, i ^ 1) for i in range(n)]
    rows = inputs.shape[0]

    def step(x):
        return lax.ppermute(x, "gx", along)

    def swap(x):
        return lax.ppermute(x, "gx", across)

    def other_core(x):
        return lax.ppermute(x, "gy", [(0, 1), (1, 0)])

    def gather(x):
        mine, theirs = [x], [swap(x)]
        for _ in range(ring - 1):
            mine.append(step(mine[-1]))
            theirs.append(swap(mine[-1]))
        order = list(range(1, ring)) + [0]
        return [b for k in order for b in (mine[k], theirs[k])]

    in_blocks = gather(inputs)
    grad_blocks = gather(out_grad)
    x, gate_own, gate_send = gather_matmul(in_blocks, w_gate, NN, "gate")
    gate_recv = other_core(gate_send)
    up_own, up_send = matmul(x, w_up, "up")
    up_recv = other_core(up_send)
    grad, back_own, back_send = gather_matmul(grad_blocks, w_down, NT, "hidden_grad")
    back_recv = other_core(back_send)
    pre = (gate_own, gate_recv, up_own, up_recv, back_own, back_recv)
    chunks = 2 if ring % 2 == 0 else 1
    blocks, saved = [], []
    for c in range(chunks):
        out = backward(pre, w_gate, w_up, c, chunks, rows, f"back{c}")
        blocks += out[:-3]
        saved.append(out[-3:])
    hidden, gate_back, up_back = zip(*saved)

    total = None
    for k in range(ring):
        part = blocks[2 * k].astype(F32) + swap(blocks[2 * k + 1]).astype(F32)
        if total is not None:
            part = part + total.astype(F32)
        total = part.astype(BF)
        if k < ring - 1:
            total = step(total)
    gate_wgrad, up_wgrad = weight_grads(x, (gate_back, up_back), "in_wgrads")
    down_wgrad = down_grads(hidden, grad, "down_wgrad")
    return (total, gate_wgrad, up_wgrad, down_wgrad)


def swiglu_back(gate_pre, up_pre, hidden_grad):
    sig = jax.nn.sigmoid(gate_pre)
    silu_val = gate_pre * sig
    hidden = (silu_val * up_pre).astype(BF)
    gate_back = (hidden_grad * up_pre * sig * (1.0 + gate_pre * (1.0 - sig))).astype(BF)
    up_back = (hidden_grad * silu_val).astype(BF)
    return (hidden, gate_back, up_back)


def plain_body(inputs, out_grad, w_gate, w_up, w_down):
    gathered_in = lax.all_gather(inputs, "gx", axis=0, tiled=True)
    gathered_grad = lax.all_gather(out_grad, "gx", axis=0, tiled=True)
    parts = (dot(gathered_in, w_gate, NN), dot(gathered_in, w_up, NN), dot(gathered_grad, w_down, NT))
    hidden, gate_back, up_back = swiglu_back(*lax.psum(parts, "gy"))
    down_wgrad = dot(hidden, gathered_grad, TN).astype(BF)
    gate_wgrad = dot(gathered_in, gate_back, TN).astype(BF)
    up_wgrad = dot(gathered_in, up_back, TN).astype(BF)
    result = dot(gate_back, w_gate, NT) + dot(up_back, w_up, NT)
    summed = lax.psum_scatter(result, "gx", scatter_dimension=0, tiled=True)
    return (summed.astype(BF), gate_wgrad, up_wgrad, down_wgrad)


def solution(mesh):
    n = mesh.shape["gx"]

    def body(inputs, out_grad, w_gate, w_up, w_down):
        args = (inputs, out_grad, w_gate, w_up, w_down)
        if n % 2 == 0 and n > 2 and mesh.shape["gy"] == 2 and inputs.shape[0] % 16 == 0:
            return ring_body(n, *args)
        return plain_body(*args)

    in_specs = (
        P(("groups", "gx"), "gy"),
        P(("groups", "gx"), "gy"),
        P("gy", "gx"),
        P("gy", "gx"),
        P("gx", "gy"),
    )
    out_specs = (
        P(("groups", "gx"), "gy"),
        P(("groups", "gy"), "gx"),
        P(("groups", "gy"), "gx"),
        P(("groups", "gx"), "gy"),
    )
    return jax.shard_map(body, mesh=mesh, in_specs=in_specs, out_specs=out_specs, check_vma=False)
```

time: 422 us -> 253 us (0.60)
  waiting for transfers between devices: 237 us -> 102 us
  matrix products: 126 us -> 0 us
  Pallas kernels: 0 us -> 121 us
  local copies, waits for them, and re-layouts: 37.4 us -> 2.17 us
  starting transfers between devices: 0.34 us -> 24 us
  between operations: 13.8 us -> 0.86 us
  other arithmetic: 7.17 us -> 2.53 us
    dot_general x8 -> x0, matrix products: 126 us -> none  [the longest x1 26.5 us: body(): lax.dot_general(up_back, w_up, contract_last, preferred_element_type=jnp....]
    all_gather x2 -> x0, waiting for transfers between devices: 122 us -> none  [the longest x1 77.6 us: body(): lax.all_gather(inputs, 'gx', axis=0, tiled=True)]
    pallas_call x0 -> x7, Pallas kernels: none -> 121 us  [the longest x2 39 us: backward(): call(kernel, name, 4 * part * depth * width, 4 * depth * width, grid=(dep...]
    ppermute x0 -> x24, waiting for transfers between devices: none -> 102 us  [the longest x9 54.5 us: step(): return lax.ppermute(x, 'gx', along)]
    reduce_scatter x1 -> x0, waiting for transfers between devices: 71.3 us -> none  [body(): lax.psum_scatter(result + lax.dot_general(up_back, w_up, contract_last, p...]
    psum x1 -> x0, waiting for transfers between devices: 42.1 us -> none  [body(): lax.psum((gate_part, up_part, back_part), 'gy')]
    unnamed x6 -> x34, local copies, waits for them, and re-layouts: 37.4 us -> 2.17 us
    ppermute x0 -> x24, starting transfers between devices: none -> 24 us  [the longest x12 13.7 us: swap(): return lax.ppermute(x, 'gx', across)]
  transfers between devices with their start and end apart: 4 -> 24, of which waited for: 4 -> 12; matrix products, arithmetic and copies ran while one was open for 26% -> 1% of each run, Pallas kernels for 0% -> 40%
where the time goes in v1:
time: 253 us; the launch traced here: 252 us
  Pallas kernels  121 us (48%)
  waiting for transfers between devices  102 us (40%)
  starting transfers between devices  24 us (9%)
    ppermute x9, waiting for transfers between devices, step(): return lax.ppermute(x, 'gx', along)  54.5 us
    ppermute x12, waiting for transfers between devices, swap(): return lax.ppermute(x, 'gx', across)  43.2 us
    pallas_call x2, Pallas kernels, backward(): call(kernel, name, 4 * part * depth * width, 4 * depth * width, grid=(dep...  39 us
    pallas_call x2, Pallas kernels, gather_matmul(): call(kernel, name, 2 * tokens * depth * width, 2 * depth * width, grid=(w...  33.4 us
    pallas_call x1, Pallas kernels, weight_grads(): call(kernel, name, 2 * tokens * depth * width * count, 2 * depth * width...  21.4 us
    pallas_call x1, Pallas kernels, matmul(): call(kernel, name, 2 * tokens * depth * width, 2 * depth * width, grid=(w...  14.5 us
    ppermute x12, starting transfers between devices, swap(): return lax.ppermute(x, 'gx', across)  13.7 us
    pallas_call x1, Pallas kernels, down_grads(): call(kernel, name, 2 * tokens * depth * width, 2 * depth * width, grid=(w...  12.8 us
  transfers between devices with their start and end apart: 24, of which 12 were waited for; matrix products, arithmetic and copies ran while one was open for 1% of the time, Pallas kernels for 40%

profile of v1, /device:TPU:0, one launch (start us, length us, event | category | flops | bytes accessed | tf_op | source)
XLA Modules:
  0.0 252.3 jit_solution(5642476892341859981)
XLA Ops:
  0.6 3.1 %collective-permute-start = (bf16[64,4096]{1,0:T(8,128)(2,1)}, bf16[64,4096]{1,0:T(8,128)(2,1)S(1)}, u32[]{:S(2)}, u32[]{:S(2)}) collective-permute-start(bf16[64,4096]{1,0:T(8,128)(2,1)} %refs_6_.4), channel_id=1, source_target_pairs={{0,4},{2,6},{4,8},{6,10},{8,12},{10,14},{12,0},{14,2},{1,5},{3,7},... | collective-permute-start | bytes 1572872 | tf_op jit(solution)/shard_map/ppermute | solution.py:241
  3.7 1.6 collective-permute-start.9
  5.3 13.4 %collective-permute-done.refs_0_ = bf16[64,4096]{1,0:T(8,128)(2,1)S(1)} collective-permute-done((bf16[64,4096]{1,0:T(8,128)(2,1)}, bf16[64,4096]{1,0:T(8,128)(2,1)S(1)}, u32[]{:S(2)}, u32[]{:S(2)}) %collective-permute-start) | collective-permute-done | bytes 524320 | tf_op jit(solution)/shard_map/ppermute | solution.py:241
  18.7 11.2 %collective-permute-done.9.refs_0_ = bf16[64,4096]{1,0:T(8,128)(2,1)S(1)} collective-permute-done((bf16[64,4096]{1,0:T(8,128)(2,1)}, bf16[64,4096]{1,0:T(8,128)(2,1)S(1)}, u32[]{:S(2)}, u32[]{:S(2)}) %collective-permute-start.9) | collective-permute-done | bytes 524320 | tf_op jit(solution)/shard_map/ppermute | solution.py:241
  30.0 11.2 %collective-permute-done.2.refs_2_ = bf16[64,4096]{1,0:T(8,128)(2,1)S(1)} collective-permute-done((bf16[64,4096]{1,0:T(8,128)(2,1)S(1)}, bf16[64,4096]{1,0:T(8,128)(2,1)S(1)}, u32[]{:S(2)}, u32[]{:S(2)}) %collective-permute-start.2) | collective-permute-done | bytes 524320 | tf_op jit(solution)/shard_map/ppermute | solution.py:241
  41.2 1.7 collective-permute-start.6
  43.2 1.7 collective-permute-start.3
  45.0 7.4 %collective-permute-done.11.refs_2_ = bf16[64,4096]{1,0:T(8,128)(2,1)S(1)} collective-permute-done((bf16[64,4096]{1,0:T(8,128)(2,1)S(1)}, bf16[64,4096]{1,0:T(8,128)(2,1)S(1)}, u32[]{:S(2)}, u32[]{:S(2)}) %collective-permute-start.11) | collective-permute-done | bytes 524320 | tf_op jit(solution)/shard_map/ppermute | solution.py:241
  52.4 11.2 %collective-permute-done.4.refs_4_ = bf16[64,4096]{1,0:T(8,128)(2,1)S(1)} collective-permute-done((bf16[64,4096]{1,0:T(8,128)(2,1)S(1)}, bf16[64,4096]{1,0:T(8,128)(2,1)S(1)}, u32[]{:S(2)}, u32[]{:S(2)}) %collective-permute-start.4) | collective-permute-done | bytes 524320 | tf_op jit(solution)/shard_map/ppermute | solution.py:241
  63.6 1.8 collective-permute-start.5
  65.7 1.8 collective-permute-done.1.refs_1_
  67.5 1.7 collective-permute-start.10
  69.2 9.5 %collective-permute-done.3.refs_3_ = bf16[64,4096]{1,0:T(8,128)(2,1)S(1)} collective-permute-done((bf16[64,4096]{1,0:T(8,128)(2,1)S(1)}, bf16[64,4096]{1,0:T(8,128)(2,1)S(1)}, u32[]{:S(2)}, u32[]{:S(2)}) %collective-permute-start.3) | collective-permute-done | bytes 524320 | tf_op jit(solution)/shard_map/ppermute | solution.py:244
  78.7 1.7 collective-permute-start.12
  80.8 9.2 %collective-permute-done.5.refs_5_ = bf16[64,4096]{1,0:T(8,128)(2,1)S(1)} collective-permute-done((bf16[64,4096]{1,0:T(8,128)(2,1)S(1)}, bf16[64,4096]{1,0:T(8,128)(2,1)S(1)}, u32[]{:S(2)}, u32[]{:S(2)}) %collective-permute-start.5) | collective-permute-done | bytes 524320 | tf_op jit(solution)/shard_map/ppermute | solution.py:244
  90.8 16.7 %gate.1 = (bf16[512,4096]{1,0:T(8,128)(2,1)}, f32[512,1792]{1,0:T(8,128)}, bf16[512,1792]{1,0:T(8,128)(2,1)}) custom-call(bf16[64,4096]{1,0:T(8,128)(2,1)} %copy-done.8, bf16[64,4096]{1,0:T(8,128)(2,1)} %copy-done.14, bf16[64,4096]{1,0:T(8,128)(2,1)} %copy-done.10, bf16[64,4096]{1,0:T(8,128)(2,1)} %copy-done.15, bf16[64,4096]{1,0:T(8,128)(2,1)} %copy-done.12, ...), custom_call_target="tpu_custom_call" | custom-call | flops 7516192768 | bytes 14680064 | tf_op jit(solution)/shard_map/gate/pallas_call | solution.py:68
  107.6 14.5 %up.1 = (f32[512,1792]{1,0:T(8,128)}, bf16[512,1792]{1,0:T(8,128)(2,1)}) custom-call(bf16[512,4096]{1,0:T(8,128)(2,1)} %get-tuple-element.30.x_ref.refs_0_, bf16[4096,1792]{1,0:T(8,128)(2,1)} %refs_7_.3), custom_call_target="tpu_custom_call" | custom-call | flops 7516192768 | bytes 14680064 | tf_op jit(solution)/shard_map/up/pallas_call | solution.py:99
  122.7 1.1 collective-permute-done.12.refs_3_
  123.8 8.6 %collective-permute-done.14.refs_5_ = bf16[64,4096]{1,0:T(8,128)(2,1)} collective-permute-done((bf16[64,4096]{1,0:T(8,128)(2,1)S(1)}, bf16[64,4096]{1,0:T(8,128)(2,1)}, u32[]{:S(2)}, u32[]{:S(2)}) %collective-permute-start.14) | collective-permute-done | bytes 524320 | tf_op jit(solution)/shard_map/ppermute | solution.py:244
  132.4 16.8 %hidden_grad.1 = (bf16[512,4096]{1,0:T(8,128)(2,1)}, f32[512,1792]{1,0:T(8,128)}, bf16[512,1792]{1,0:T(8,128)(2,1)}) custom-call(bf16[64,4096]{1,0:T(8,128)(2,1)} %copy-done.6, bf16[64,4096]{1,0:T(8,128)(2,1)} %collective-permute-done.10.refs_1_, bf16[64,4096]{1,0:T(8,128)(2,1)} %copy-done.7, bf16[64,4096]{1,0:T(8,128)(2,1)} %collective-permute-done.12.refs_3_, ...), custom_call_target="tpu_custom_call" | custom-call | flops 7516192768 | bytes 14680064 | tf_op jit(solution)/shard_map/hidden_grad/pallas_call | solution.py:68
  149.3 3.9 %collective-permute-done.16.refs_5_ = bf16[512,1792]{1,0:T(8,128)(2,1)S(1)} collective-permute-done((bf16[512,1792]{1,0:T(8,128)(2,1)}, bf16[512,1792]{1,0:T(8,128)(2,1)S(1)}, u32[]{:S(2)}, u32[]{:S(2)}) %collective-permute-start.16) | collective-permute-done | bytes 1835040 | tf_op jit(solution)/shard_map/ppermute | solution.py:247
  153.3 1.3 copy-done.2
  154.5 19.5 %back0.1 = (bf16[64,4096]{1,0:T(8,128)(2,1)}, bf16[64,4096]{1,0:T(8,128)(2,1)}, bf16[64,4096]{1,0:T(8,128)(2,1)}, bf16[64,4096]{1,0:T(8,128)(2,1)}, bf16[256,179...) custom-call(f32[512,1792]{1,0:T(8,128)} %get-tuple-element.28.refs_0_, ...), custom_call_target="tpu_custom_call" | custom-call | flops 7516192768 | bytes 29360128 | tf_op jit(solution)/shard_map/back0/pallas_call | solution.py:150
  174.1 1.3 collective-permute-start.20
  176.2 13.0 %collective-permute-done.20 = bf16[64,4096]{1,0:T(8,128)(2,1)S(1)} collective-permute-done((bf16[64,4096]{1,0:T(8,128)(2,1)}, bf16[64,4096]{1,0:T(8,128)(2,1)S(1)}, u32[]{:S(2)}, u32[]{:S(2)}) %collective-permute-start.20) | collective-permute-done | bytes 524320 | tf_op jit(solution)/shard_map/ppermute | solution.py:244
  189.1 1.2 add_convert_fusion.3
  191.1 19.5 %back1.1 = (bf16[64,4096]{1,0:T(8,128)(2,1)}, bf16[64,4096]{1,0:T(8,128)(2,1)}, bf16[64,4096]{1,0:T(8,128)(2,1)}, bf16[64,4096]{1,0:T(8,128)(2,1)}, bf16[256,179...) custom-call(f32[512,1792]{1,0:T(8,128)} %get-tuple-element.28.refs_0_, ...), custom_call_target="tpu_custom_call" | custom-call | flops 7516192768 | bytes 29360128 | tf_op jit(solution)/shard_map/back1/pallas_call | solution.py:150
  210.5 1.6 collective-permute-start.18
  212.8 1.6 collective-permute-start.22
  214.5 21.4 %in_wgrads.1 = (bf16[4096,1792]{1,0:T(8,128)(2,1)}, bf16[4096,1792]{1,0:T(8,128)(2,1)}) custom-call(bf16[512,4096]{1,0:T(8,128)(2,1)} %get-tuple-element.30.x_ref.refs_0_, bf16[256,1792]{1,0:T(8,128)(2,1)} %get-tuple-element.43.refs_1_, bf16[256,1792]{1,0:T(8,128)(2,1)} %get-tuple-element.44.refs_2_, bf16[256,1792]{1,0:T(8,128)(2,1)} %get-tuple-element.45.refs_3_, ...), custom_call_target="tpu_custom_call" | custom-call | flops 15032385536 | bytes 29360128 | tf_op jit(solution)/shard_map/in_wgrads/pallas_call | solution.py:195
  236.1 2.4 collective-permute-start.23
  238.5 12.8 %down_wgrad.1 = bf16[1792,4096]{1,0:T(8,128)(2,1)} custom-call(bf16[256,1792]{1,0:T(8,128)(2,1)} %get-tuple-element.49.refs_0_, bf16[256,1792]{1,0:T(8,128)(2,1)} %get-tuple-element.50.refs_1_, bf16[512,4096]{1,0:T(8,128)(2,1)} %get-tuple-element.51.refs_2_), custom_call_target="tpu_custom_call" | custom-call | flops 7516192768 | bytes 14680064 | tf_op jit(solution)/shard_map/down_wgrad/pallas_call | solution.py:221
  (61 shorter events, 5.9 us)
Async XLA Ops:
  0.6 18.1 %collective-permute-start = (bf16[64,4096]{1,0:T(8,128)(2,1)}, bf16[64,4096]{1,0:T(8,128)(2,1)S(1)}, u32[]{:S(2)}, u32[]{:S(2)}) collective-permute-start(bf16[64,4096]{1,0:T(8,128)(2,1)} %refs_6_.4), channel_id=1, source_target_pairs={{0,4},{2,6},{4,8},{6,10},{8,12},{10,14},{12,0},{14,2},{1,5},{3,7},... | collective-permute-start | bytes 1572872 | tf_op jit(solution)/shard_map/ppermute | solution.py:241
  3.7 26.2 %collective-permute-start.9 = (bf16[64,4096]{1,0:T(8,128)(2,1)}, bf16[64,4096]{1,0:T(8,128)(2,1)S(1)}, u32[]{:S(2)}, u32[]{:S(2)}) collective-permute-start(bf16[64,4096]{1,0:T(8,128)(2,1)} %refs_6_.5), channel_id=1, source_target_pairs={{0,4},{2,6},{4,8},{6,10},{8,12},{10,14},{12,0},{14,2},{1,5},{3,7},... | collective-permute-start | bytes 1572872 | tf_op jit(solution)/shard_map/ppermute | solution.py:241
  18.7 71.3 %copy-start.8 = (bf16[64,4096]{1,0:T(8,128)(2,1)}, bf16[64,4096]{1,0:T(8,128)(2,1)S(1)}, u32[]{:S(2)}) copy-start(bf16[64,4096]{1,0:T(8,128)(2,1)S(1)} %collective-permute-done.refs_0_) | copy-start | bytes 1572868
  18.7 22.5 %collective-permute-start.2 = (bf16[64,4096]{1,0:T(8,128)(2,1)S(1)}, bf16[64,4096]{1,0:T(8,128)(2,1)S(1)}, u32[]{:S(2)}, u32[]{:S(2)}) collective-permute-start(bf16[64,4096]{1,0:T(8,128)(2,1)S(1)} %collective-permute-done.refs_0_), channel_id=1, source_target_pairs={{0,4},{2,6},{4,8},{6,10},{8,12},{10,14},{12,0},{14,2},{1,5},{3,7},... | collective-permute-start | bytes 1572872 | tf_op jit(solution)/shard_map/ppermute | solution.py:241
  29.9 77.6 %copy-start.6 = (bf16[64,4096]{1,0:T(8,128)(2,1)}, bf16[64,4096]{1,0:T(8,128)(2,1)S(1)}, u32[]{:S(2)}) copy-start(bf16[64,4096]{1,0:T(8,128)(2,1)S(1)} %collective-permute-done.9.refs_0_) | copy-start | bytes 1572868
  29.9 22.5 %collective-permute-start.11 = (bf16[64,4096]{1,0:T(8,128)(2,1)S(1)}, bf16[64,4096]{1,0:T(8,128)(2,1)S(1)}, u32[]{:S(2)}, u32[]{:S(2)}) collective-permute-start(bf16[64,4096]{1,0:T(8,128)(2,1)S(1)} %collective-permute-done.9.refs_0_), channel_id=1, source_target_pairs={{0,4},{2,6},{4,8},{6,10},{8,12},{10,14},{12,0},{14,2},{1,5},{3,7},... | collective-permute-start | bytes 1572872 | tf_op jit(solution)/shard_map/ppermute | solution.py:241
  41.2 48.8 %copy-start.10 = (bf16[64,4096]{1,0:T(8,128)(2,1)}, bf16[64,4096]{1,0:T(8,128)(2,1)S(1)}, u32[]{:S(2)}) copy-start(bf16[64,4096]{1,0:T(8,128)(2,1)S(1)} %collective-permute-done.2.refs_2_) | copy-start | bytes 1572868
  41.2 22.5 %collective-permute-start.4 = (bf16[64,4096]{1,0:T(8,128)(2,1)S(1)}, bf16[64,4096]{1,0:T(8,128)(2,1)S(1)}, u32[]{:S(2)}, u32[]{:S(2)}) collective-permute-start(bf16[64,4096]{1,0:T(8,128)(2,1)S(1)} %collective-permute-done.2.refs_2_), channel_id=1, source_target_pairs={{0,4},{2,6},{4,8},{6,10},{8,12},{10,14},{12,0},{14,2},{1,5},{3,7},... | collective-permute-start | bytes 1572872 | tf_op jit(solution)/shard_map/ppermute | solution.py:241
  41.2 24.2 %collective-permute-start.6 = (bf16[64,4096]{1,0:T(8,128)(2,1)}, bf16[64,4096]{1,0:T(8,128)(2,1)S(1)}, u32[]{:S(2)}, u32[]{:S(2)}) collective-permute-start(bf16[64,4096]{1,0:T(8,128)(2,1)} %refs_6_.4), channel_id=1, source_target_pairs={{0,2},{2,0},{4,6},{6,4},{8,10},{10,8},{12,14},{14,12},{1,3},{3,1},... | collective-permute-start | bytes 1572872 | tf_op jit(solution)/shard_map/ppermute | solution.py:244
  42.9 24.6 %collective-permute-start.1 = (bf16[64,4096]{1,0:T(8,128)(2,1)S(1)}, bf16[64,4096]{1,0:T(8,128)(2,1)S(1)}, u32[]{:S(2)}, u32[]{:S(2)}) collective-permute-start(bf16[64,4096]{1,0:T(8,128)(2,1)S(1)} %collective-permute-done.refs_0_), channel_id=1, source_target_pairs={{0,2},{2,0},{4,6},{6,4},{8,10},{10,8},{12,14},{14,12},{1,3},{3,1},... | collective-permute-start | bytes 1572872 | tf_op jit(solution)/shard_map/ppermute | solution.py:244
  43.2 35.5 %collective-permute-start.3 = (bf16[64,4096]{1,0:T(8,128)(2,1)S(1)}, bf16[64,4096]{1,0:T(8,128)(2,1)S(1)}, u32[]{:S(2)}, u32[]{:S(2)}) collective-permute-start(bf16[64,4096]{1,0:T(8,128)(2,1)S(1)} %collective-permute-done.2.refs_2_), channel_id=1, source_target_pairs={{0,2},{2,0},{4,6},{6,4},{8,10},{10,8},{12,14},{14,12},{1,3},{3,1},... | collective-permute-start | bytes 1572872 | tf_op jit(solution)/shard_map/ppermute | solution.py:244
  52.4 55.1 %copy-start.7 = (bf16[64,4096]{1,0:T(8,128)(2,1)}, bf16[64,4096]{1,0:T(8,128)(2,1)S(1)}, u32[]{:S(2)}) copy-start(bf16[64,4096]{1,0:T(8,128)(2,1)S(1)} %collective-permute-done.11.refs_2_) | copy-start | bytes 1572868
  52.4 28.1 %collective-permute-start.13 = (bf16[64,4096]{1,0:T(8,128)(2,1)S(1)}, bf16[64,4096]{1,0:T(8,128)(2,1)S(1)}, u32[]{:S(2)}, u32[]{:S(2)}) collective-permute-start(bf16[64,4096]{1,0:T(8,128)(2,1)S(1)} %collective-permute-done.11.refs_2_), channel_id=1, source_target_pairs={{0,4},{2,6},{4,8},{6,10},{8,12},{10,14},{12,0},{14,2},{1,5},{3,7},... | collective-permute-start | bytes 1572872 | tf_op jit(solution)/shard_map/ppermute | solution.py:241
  63.6 26.4 %copy-start.12 = (bf16[64,4096]{1,0:T(8,128)(2,1)}, bf16[64,4096]{1,0:T(8,128)(2,1)S(1)}, u32[]{:S(2)}) copy-start(bf16[64,4096]{1,0:T(8,128)(2,1)S(1)} %collective-permute-done.4.refs_4_) | copy-start | bytes 1572868
  63.6 26.3 %collective-permute-start.5 = (bf16[64,4096]{1,0:T(8,128)(2,1)S(1)}, bf16[64,4096]{1,0:T(8,128)(2,1)S(1)}, u32[]{:S(2)}, u32[]{:S(2)}) collective-permute-start(bf16[64,4096]{1,0:T(8,128)(2,1)S(1)} %collective-permute-done.4.refs_4_), channel_id=1, source_target_pairs={{0,2},{2,0},{4,6},{6,4},{8,10},{10,8},{12,14},{14,12},{1,3},{3,1},... | collective-permute-start | bytes 1572872 | tf_op jit(solution)/shard_map/ppermute | solution.py:244
  65.4 24.6 %copy-start.13 = (bf16[64,4096]{1,0:T(8,128)(2,1)}, bf16[64,4096]{1,0:T(8,128)(2,1)S(1)}, u32[]{:S(2)}) copy-start(bf16[64,4096]{1,0:T(8,128)(2,1)S(1)} %collective-permute-done.6.refs_7_) | copy-start | bytes 1572868
  65.4 56.8 %collective-permute-start.15 = (bf16[64,4096]{1,0:T(8,128)(2,1)}, bf16[64,4096]{1,0:T(8,128)(2,1)S(1)}, u32[]{:S(2)}, u32[]{:S(2)}) collective-permute-start(bf16[64,4096]{1,0:T(8,128)(2,1)} %refs_6_.5), channel_id=1, source_target_pairs={{0,2},{2,0},{4,6},{6,4},{8,10},{10,8},{12,14},{14,12},{1,3},{3,1},... | collective-permute-start | bytes 1572872 | tf_op jit(solution)/shard_map/ppermute | solution.py:244
  67.5 22.5 %copy-start.14 = (bf16[64,4096]{1,0:T(8,128)(2,1)}, bf16[64,4096]{1,0:T(8,128)(2,1)S(1)}, u32[]{:S(2)}) copy-start(bf16[64,4096]{1,0:T(8,128)(2,1)S(1)} %collective-permute-done.1.refs_1_) | copy-start | bytes 1572868
  67.5 55.2 %collective-permute-start.10 = (bf16[64,4096]{1,0:T(8,128)(2,1)S(1)}, bf16[64,4096]{1,0:T(8,128)(2,1)}, u32[]{:S(2)}, u32[]{:S(2)}) collective-permute-start(bf16[64,4096]{1,0:T(8,128)(2,1)S(1)} %collective-permute-done.9.refs_0_), channel_id=1, source_target_pairs={{0,2},{2,0},{4,6},{6,4},{8,10},{10,8},{12,14},{14,12},{1,3},{3,1},... | collective-permute-start | bytes 1572872 | tf_op jit(solution)/shard_map/ppermute | solution.py:244
  78.7 45.0 %collective-permute-start.12 = (bf16[64,4096]{1,0:T(8,128)(2,1)S(1)}, bf16[64,4096]{1,0:T(8,128)(2,1)}, u32[]{:S(2)}, u32[]{:S(2)}) collective-permute-start(bf16[64,4096]{1,0:T(8,128)(2,1)S(1)} %collective-permute-done.11.refs_2_), channel_id=1, source_target_pairs={{0,2},{2,0},{4,6},{6,4},{8,10},{10,8},{12,14},{14,12},{1,3},{3,1},... | collective-permute-start | bytes 1572872 | tf_op jit(solution)/shard_map/ppermute | solution.py:244
  80.5 27.1 %copy-start.9 = (bf16[64,4096]{1,0:T(8,128)(2,1)}, bf16[64,4096]{1,0:T(8,128)(2,1)S(1)}, u32[]{:S(2)}) copy-start(bf16[64,4096]{1,0:T(8,128)(2,1)S(1)} %collective-permute-done.13.refs_4_) | copy-start | bytes 1572868
  80.5 51.9 %collective-permute-start.14 = (bf16[64,4096]{1,0:T(8,128)(2,1)S(1)}, bf16[64,4096]{1,0:T(8,128)(2,1)}, u32[]{:S(2)}, u32[]{:S(2)}) collective-permute-start(bf16[64,4096]{1,0:T(8,128)(2,1)S(1)} %collective-permute-done.13.refs_4_), channel_id=1, source_target_pairs={{0,2},{2,0},{4,6},{6,4},{8,10},{10,8},{12,14},{14,12},{1,3},{3,1},... | collective-permute-start | bytes 1572872 | tf_op jit(solution)/shard_map/ppermute | solution.py:244
  107.5 41.7 %collective-permute-start.7 = (bf16[512,1792]{1,0:T(8,128)(2,1)}, bf16[512,1792]{1,0:T(8,128)(2,1)S(1)}, u32[]{:S(2)}, u32[]{:S(2)}) collective-permute-start(bf16[512,1792]{1,0:T(8,128)(2,1)} %get-tuple-element.29), channel_id=1, source_target_pairs={{0,1},{1,0},{2,3},{3,2},{4,5},{5,4},{6,7},{7,6},{8,9},{9,8},{10,11... | collective-permute-start | bytes 5505032 | tf_op jit(solution)/shard_map/ppermute | solution.py:247
  122.2 27.1 %collective-permute-start.8 = (bf16[512,1792]{1,0:T(8,128)(2,1)}, bf16[512,1792]{1,0:T(8,128)(2,1)S(1)}, u32[]{:S(2)}, u32[]{:S(2)}) collective-permute-start(bf16[512,1792]{1,0:T(8,128)(2,1)} %get-tuple-element.32), channel_id=1, source_target_pairs={{0,1},{1,0},{2,3},{3,2},{4,5},{5,4},{6,7},{7,6},{8,9},{9,8},{10,11... | collective-permute-start | bytes 5505032 | tf_op jit(solution)/shard_map/ppermute | solution.py:247
  149.2 4.1 %collective-permute-start.16 = (bf16[512,1792]{1,0:T(8,128)(2,1)}, bf16[512,1792]{1,0:T(8,128)(2,1)S(1)}, u32[]{:S(2)}, u32[]{:S(2)}) collective-permute-start(bf16[512,1792]{1,0:T(8,128)(2,1)} %get-tuple-element.34), channel_id=1, source_target_pairs={{0,1},{1,0},{2,3},{3,2},{4,5},{5,4},{6,7},{7,6},{8,9},{9,8},{10,11... | collective-permute-start | bytes 5505032 | tf_op jit(solution)/shard_map/ppermute | solution.py:247
  174.1 15.0 %collective-permute-start.20 = (bf16[64,4096]{1,0:T(8,128)(2,1)}, bf16[64,4096]{1,0:T(8,128)(2,1)S(1)}, u32[]{:S(2)}, u32[]{:S(2)}) collective-permute-start(bf16[64,4096]{1,0:T(8,128)(2,1)} %get-tuple-element.42), channel_id=1, source_target_pairs={{0,2},{2,0},{4,6},{6,4},{8,10},{10,8},{12,14},{14,12},{1,3},{3,1},... | collective-permute-start | bytes 1572872 | tf_op jit(solution)/shard_map/ppermute | solution.py:244
  175.4 37.2 %collective-permute-start.19 = (bf16[64,4096]{1,0:T(8,128)(2,1)}, bf16[64,4096]{1,0:T(8,128)(2,1)S(1)}, u32[]{:S(2)}, u32[]{:S(2)}) collective-permute-start(bf16[64,4096]{1,0:T(8,128)(2,1)} %get-tuple-element.40), channel_id=1, source_target_pairs={{0,2},{2,0},{4,6},{6,4},{8,10},{10,8},{12,14},{14,12},{1,3},{3,1},... | collective-permute-start | bytes 1572872 | tf_op jit(solution)/shard_map/ppermute | solution.py:244
  190.3 22.3 %collective-permute-start.21 = (bf16[64,4096]{1,0:T(8,128)(2,1)S(1)}, bf16[64,4096]{1,0:T(8,128)(2,1)S(1)}, u32[]{:S(2)}, u32[]{:S(2)}) collective-permute-start(bf16[64,4096]{1,0:T(8,128)(2,1)S(1)} %add_convert_fusion.3), channel_id=1, source_target_pairs={{0,4},{2,6},{4,8},{6,10},{8,12},{10,14},{12,0},{14,2},{1,5},{3,7},... | collective-permute-start | bytes 1572872 | tf_op jit(solution)/shard_map/ppermute | solution.py:241
  210.5 25.3 %collective-permute-start.18 = (bf16[64,4096]{1,0:T(8,128)(2,1)}, bf16[64,4096]{1,0:T(8,128)(2,1)S(1)}, u32[]{:S(2)}, u32[]{:S(2)}) collective-permute-start(bf16[64,4096]{1,0:T(8,128)(2,1)} %get-tuple-element.38), channel_id=1, source_target_pairs={{0,2},{2,0},{4,6},{6,4},{8,10},{10,8},{12,14},{14,12},{1,3},{3,1},... | collective-permute-start | bytes 1572872 | tf_op jit(solution)/shard_map/ppermute | solution.py:244
  212.1 39.2 %collective-permute-start.17 = (bf16[64,4096]{1,0:T(8,128)(2,1)}, bf16[64,4096]{1,0:T(8,128)(2,1)S(1)}, u32[]{:S(2)}, u32[]{:S(2)}) collective-permute-start(bf16[64,4096]{1,0:T(8,128)(2,1)} %get-tuple-element.36), channel_id=1, source_target_pairs={{0,2},{2,0},{4,6},{6,4},{8,10},{10,8},{12,14},{14,12},{1,3},{3,1},... | collective-permute-start | bytes 1572872 | tf_op jit(solution)/shard_map/ppermute | solution.py:244
  212.8 23.1 %collective-permute-start.22 = (bf16[64,4096]{1,0:T(8,128)(2,1)S(1)}, bf16[64,4096]{1,0:T(8,128)(2,1)S(1)}, u32[]{:S(2)}, u32[]{:S(2)}) collective-permute-start(bf16[64,4096]{1,0:T(8,128)(2,1)S(1)} %add_convert_fusion.2), channel_id=1, source_target_pairs={{0,4},{2,6},{4,8},{6,10},{8,12},{10,14},{12,0},{14,2},{1,5},{3,7},... | collective-permute-start | bytes 1572872 | tf_op jit(solution)/shard_map/ppermute | solution.py:241
  236.1 15.2 %collective-permute-start.23 = (bf16[64,4096]{1,0:T(8,128)(2,1)S(1)}, bf16[64,4096]{1,0:T(8,128)(2,1)S(1)}, u32[]{:S(2)}, u32[]{:S(2)}) collective-permute-start(bf16[64,4096]{1,0:T(8,128)(2,1)S(1)} %add_convert_fusion.1), channel_id=1, source_target_pairs={{0,4},{2,6},{4,8},{6,10},{8,12},{10,14},{12,0},{14,2},{1,5},{3,7},... | collective-permute-start | bytes 1572872 | tf_op jit(solution)/shard_map/ppermute | solution.py:241
  (9 other events, 88.1 us)

commit v2 on v0

v2 whole, which is shorter than its diff:
```python
import jax
import jax.numpy as jnp
from jax import lax
from jax.experimental import pallas as pl
from jax.experimental.pallas import tpu as pltpu
from jax.sharding import PartitionSpec as P

BF = jnp.bfloat16
F32 = jnp.float32
ANY_SPEC = pl.BlockSpec(memory_space=pl.ANY)
HBM_SPEC = pl.BlockSpec(memory_space=pltpu.HBM)
VMEM_SPEC = pl.BlockSpec(memory_space=pltpu.VMEM)
NN = (((1,), (0,)), ((), ()))
NT = (((1,), (1,)), ((), ()))
TN = (((0,), (0,)), ((), ()))


def dot(a, b, dims):
    return lax.dot_general(a, b, dims, preferred_element_type=F32)


def tile_of(extent, wanted):
    for tile in range(wanted, 127, -128):
        if extent % tile == 0:
            return tile
    return extent


def call(kernel, name, flops, nbytes, vmem, **kwargs):
    return pl.pallas_call(
        kernel,
        name=name,
        compiler_params=pltpu.CompilerParams(vmem_limit_bytes=vmem * 2**20),
        cost_estimate=pl.CostEstimate(flops=flops, bytes_accessed=nbytes, transcendentals=0),
        **kwargs,
    )


def run_copies(copies):
    for c in copies:
        c.start()
    for c in copies:
        c.wait()


def in_hbm(x):
    return pltpu.with_memory_space_constraint(x, pltpu.HBM)


def hold(weight, vmem, name):
    def kernel(w_ref, out_ref, sem):
        run_copies([pltpu.make_async_copy(w_ref, out_ref, sem)])

    return call(
        kernel,
        name,
        0,
        2 * weight.size,
        vmem,
        in_specs=[HBM_SPEC],
        out_specs=VMEM_SPEC,
        out_shape=pltpu.VMEM(weight.shape, BF),
        scratch_shapes=[pltpu.SemaphoreType.DMA],
    )(in_hbm(weight))


def gather_matmul(pieces, weights, dims, send_type, name):
    rows, depth = pieces[0].shape
    count, nw = len(pieces), len(weights)
    tokens = rows * count
    width = weights[0].shape[1] if dims == NN else weights[0].shape[0]
    tile = tile_of(width, 256)
    outs = 1 if send_type == F32 else 2

    def kernel(*refs):
        piece_refs, w_refs = refs[:count], refs[count : count + nw]
        x_ref, *out_refs = refs[count + nw : -1]
        sems = refs[-1]

        @pl.when(pl.program_id(0) == 0)
        def _():
            run_copies(
                [
                    pltpu.make_async_copy(p, x_ref.at[pl.ds(i * rows, rows)], sems.at[i])
                    for i, p in enumerate(piece_refs)
                ]
            )

        at = pl.ds(pl.multiple_of(pl.program_id(0) * tile, tile), tile)
        for i, w_ref in enumerate(w_refs):
            out = dot(x_ref[...], w_ref[:, at] if dims == NN else w_ref[at, :], dims)
            for ref in out_refs:
                ref[i] = out.astype(ref.dtype)

    return call(
        kernel,
        name,
        2 * tokens * depth * width * nw,
        2 * tokens * depth,
        17,
        grid=(width // tile,),
        in_specs=[ANY_SPEC] * count + [VMEM_SPEC] * nw,
        out_specs=[pl.BlockSpec((tokens, depth), lambda j: (0, 0))]
        + [pl.BlockSpec((nw, tokens, tile), lambda j: (0, 0, j))] * outs,
        out_shape=[pltpu.HBM((tokens, depth), BF)]
        + [pltpu.HBM((nw, tokens, width), t) for t in (F32, send_type)[:outs]],
        scratch_shapes=[pltpu.SemaphoreType.DMA((count,))],
    )(*pieces, *weights)


def backward(own_gu, recv_gu, own_h, recv_h, w_gate, w_up, rows, name):
    _, tokens, width = own_gu.shape
    depth = w_gate.shape[0]
    blocks = tokens // rows
    act_tile = tile_of(width, 896)
    tile = tile_of(depth, 512)
    act_steps = width // act_tile

    def kernel(*refs):
        own_gu_ref, recv_gu_ref, own_h_ref, recv_h_ref, wg_ref, wu_ref = refs[:6]
        block_refs = refs[6 : 6 + blocks]
        hidden_ref, gb_ref, ub_ref, gb_t, ub_t = refs[6 + blocks :]
        step = pl.program_id(0)

        @pl.when(step < act_steps)
        def _():
            part = tile_of(act_tile, 256)

            @pl.loop(0, act_tile // part)
            def _(i):
                at = pl.ds(pl.multiple_of(i * part, part), part)
                gate_pre = own_gu_ref[0, :, at] + recv_gu_ref[0, :, at].astype(F32)
                up_pre = own_gu_ref[1, :, at] + recv_gu_ref[1, :, at].astype(F32)
                hidden_grad = own_h_ref[0, :, at] + recv_h_ref[0, :, at].astype(F32)
                sig = jax.nn.sigmoid(gate_pre)
                silu_val = gate_pre * sig
                hidden_ref[:, at] = (silu_val * up_pre).astype(BF)
                gate_back = (hidden_grad * up_pre * sig * (1.0 + gate_pre * (1.0 - sig))).astype(BF)
                up_back = (hidden_grad * silu_val).astype(BF)
                gb_ref[:, at] = gate_back
                ub_ref[:, at] = up_back
                lines = pl.ds(pl.multiple_of(step * act_tile + i * part, part), part)
                gb_t[lines, :] = gate_back.T
                ub_t[lines, :] = up_back.T

        @pl.when(step >= act_steps)
        def _():
            at = pl.ds(pl.multiple_of((step - act_steps) * tile, tile), tile)
            out = (dot(wg_ref[at, :], gb_t[...], NN) + dot(wu_ref[at, :], ub_t[...], NN)).T
            for i, ref in enumerate(block_refs):
                ref[...] = out[i * rows : (i + 1) * rows].astype(BF)

    def act_spec(lead):
        return pl.BlockSpec((lead, tokens, act_tile), lambda j: (0, 0, jnp.minimum(j, act_steps - 1)))

    act_out = pl.BlockSpec((tokens, act_tile), lambda j: (0, jnp.minimum(j, act_steps - 1)))
    return call(
        kernel,
        name,
        4 * tokens * depth * width,
        20 * tokens * width,
        31,
        grid=(act_steps + depth // tile,),
        in_specs=[act_spec(2), act_spec(2), act_spec(1), act_spec(1), VMEM_SPEC, VMEM_SPEC],
        out_specs=[pl.BlockSpec((rows, tile), lambda j: (0, jnp.maximum(j - act_steps, 0)))] * blocks + [act_out] * 3,
        out_shape=[pltpu.HBM((rows, depth), BF)] * blocks + [pltpu.HBM((tokens, width), BF)] * 3,
        scratch_shapes=[pltpu.VMEM((width, tokens), BF)] * 2,
    )(in_hbm(own_gu), recv_gu, in_hbm(own_h), recv_h, w_gate, w_up)


def weight_grads(x_chunks, ys_chunks, wanted, name):
    pieces, count = len(x_chunks), len(ys_chunks)
    part, depth = x_chunks[0].shape
    width = ys_chunks[0][0].shape[1]
    tokens = part * pieces
    tile = tile_of(depth, wanted)

    def kernel(*refs):
        x_refs, y_refs = refs[:pieces], refs[pieces : pieces * (1 + count)]
        out_refs = refs[pieces * (1 + count) : pieces * (1 + count) + count]
        ys, sems = refs[-1 - count : -1], refs[-1]

        @pl.when(pl.program_id(0) == 0)
        def _():
            run_copies(
                [
                    pltpu.make_async_copy(
                        y_refs[k * pieces + i], ys[k].at[pl.ds(i * part, part)], sems.at[k * pieces + i]
                    )
                    for k in range(count)
                    for i in range(pieces)
                ]
            )

        x = jnp.concatenate([r[...] for r in x_refs], axis=0)
        for y, out_ref in zip(ys, out_refs):
            out_ref[...] = dot(x, y[...], TN).astype(BF)

    return call(
        kernel,
        name,
        2 * tokens * depth * width * count,
        2 * depth * width * count,
        28,
        grid=(depth // tile,),
        in_specs=[pl.BlockSpec((part, tile), lambda j: (0, j))] * pieces + [ANY_SPEC] * (pieces * count),
        out_specs=[pl.BlockSpec((tile, width), lambda j: (j, 0))] * count,
        out_shape=[pltpu.HBM((depth, width), BF)] * count,
        scratch_shapes=[pltpu.VMEM((tokens, width), BF)] * count + [pltpu.SemaphoreType.DMA((count * pieces,))],
    )(*x_chunks, *[y for ys in ys_chunks for y in ys])


def in_order(*arrays):
    return lax.optimization_barrier(arrays)


def gather_stages(ring):
    along = [f"in {k}" for k in range(1, ring)] + [f"grad {k}" for k in range(1, ring)] + [f"grad other {ring - 1}"]
    across = [f"in other {k}" for k in range(ring)] + [f"grad other {k}" for k in range(1, ring - 1)] + ["grad other 0"]
    kernels = [["gate"], ["up"]] + [[]] * (ring - 3) + [["a"], ["b"], ["down"]]
    kernels += [[]] * (len(along) - 1 - len(kernels)) + [["h_a"]]
    return [([m, s], k) for m, s, k in zip(along, across, kernels)]


def ring_body(n, inputs, out_grad, w_gate, w_up, w_down):
    ring = n // 2
    half = ring // 2
    last = ring - 1
    across = [(i, i ^ 1) for i in range(n)]
    rows = inputs.shape[0]

    def shift(x, by=1):
        pairs = [(2 * p + s, 2 * ((p + by) % ring) + s) for p in range(ring) for s in range(2)]
        return lax.ppermute(x, "gx", pairs)

    def swap(x):
        return lax.ppermute(x, "gx", across)

    def other_core(x):
        return lax.ppermute(x, "gy", [(0, 1), (1, 0)])

    order = list(range(1, ring)) + [0]
    early, late = order[:half], order[half:]
    have = {"in 0": inputs, "grad 0": out_grad, "w_gate": w_gate, "w_up": w_up, "w_down": w_down}

    def blocks_of(name, ks):
        return [b for k in ks for b in (have[f"{name} {k}"], have[f"{name} other {k}"])]

    def source(move):
        name, *other, k = move.split()
        k = int(k)
        if other and (name, k) != ("grad", last):
            return f"{name} {k}", swap
        return " ".join([name, *other, str(k - 1)]), shift

    def products(name, ks, weights, dims, tag):
        out = gather_matmul(blocks_of(name, ks), [have[w] for w in weights], dims, BF, tag)
        return dict(zip((f"{tag} x", f"{tag} own", f"{tag} send"), out))

    def gate_up(ks, tag):
        return lambda: products("in", ks, ("gate", "up"), NN, tag)

    kernels = {
        "gate": lambda: {"gate": hold(have["w_gate"], 45, "hold_gate")},
        "up": lambda: {"up": hold(have["w_up"], 31, "hold_up")},
        "down": lambda: {"down": hold(have["w_down"], 17, "hold_down")},
        "a": gate_up(early, "gu_a"),
        "b": gate_up(late, "gu_b"),
        "h_a": lambda: products("grad", early, ("down",), NT, "h_a"),
    }
    for moves, names in gather_stages(ring):
        fresh = {}
        for move in moves:
            name, how = source(move)
            fresh[move] = how(have[name])
        for name in names:
            fresh.update(kernels[name]())
        have.update(fresh)
        have = dict(zip(have, in_order(*have.values())))

    made = {"w_gate": have["gate"], "w_up": have["up"], "x_a": have["gu_a x"], "x_b": have["gu_b x"]}
    made.update(gu_a=have["gu_a own"], gu_b=have["gu_b own"], gu_send_a=have["gu_a send"], gu_send_b=have["gu_b send"])
    made.update(grad_a=have["h_a x"], h_a=have["h_a own"], h_send_a=have["h_a send"])

    gu_recv_a, gu_recv_b = other_core(made["gu_send_a"]), other_core(made["gu_send_b"])
    h_recv_a = other_core(made["h_send_a"])
    out = products("grad", late, ("down",), NT, "h_b").values()
    grad_b, h_b, h_send_b, h_a = in_order(*out, made["h_a"])
    h_recv_b = other_core(h_send_b)

    weights = (made["w_gate"], made["w_up"])
    out_a = backward(made["gu_a"], gu_recv_a, h_a, h_recv_a, *weights, rows, "back_a")
    *out_a, h_b = in_order(*out_a, h_b)
    own, sent, recv = {}, {}, {}
    for i, k in enumerate(order[:half]):
        own[k], sent[k] = out_a[2 * i : 2 * i + 2]
    for k in reversed(order[:half]):
        recv[k] = swap(sent[k])
    saved_a = out_a[-3:]
    out_b = backward(made["gu_b"], gu_recv_b, h_b, h_recv_b, *weights, rows, "back_b")
    recv[half], *out_b = in_order(recv[half], *out_b)
    for i, k in enumerate(order[half:]):
        own[k], sent[k] = out_b[2 * i : 2 * i + 2]
    saved_b = out_b[-3:]
    hidden, gate_back, up_back = zip(saved_a, saved_b)

    def add(k, *terms):
        total = own[k].astype(F32) + recv[k].astype(F32)
        for t in terms:
            total = total + t.astype(F32)
        return total.astype(BF)

    down = shift(add(half), -1)
    for k in order[half:]:
        if k:
            recv[k] = swap(sent[k])
    (down_wgrad,) = weight_grads(hidden, ((made["grad_a"], grad_b),), 256, "down_wgrad")
    out = in_order(down, recv[half - 1], recv[half + 1], sent[0], down_wgrad)
    down, recv[half - 1], recv[half + 1], sent[0], down_wgrad = out
    for k in range(half - 1, 0, -1):
        down = shift(add(k, down), -1)
    ahead = shift(add(half + 1))
    for k in range(half + 2, ring):
        ahead = shift(add(k, ahead))
    recv[0] = swap(sent[0])
    gate_wgrad, up_wgrad = weight_grads((made["x_a"], made["x_b"]), (gate_back, up_back), 512, "in_wgrads")
    input_grad = add(0, down, ahead)
    return (input_grad, gate_wgrad, up_wgrad, down_wgrad)


def swiglu_back(gate_pre, up_pre, hidden_grad):
    sig = jax.nn.sigmoid(gate_pre)
    silu_val = gate_pre * sig
    hidden = (silu_val * up_pre).astype(BF)
    gate_back = (hidden_grad * up_pre * sig * (1.0 + gate_pre * (1.0 - sig))).astype(BF)
    up_back = (hidden_grad * silu_val).astype(BF)
    return (hidden, gate_back, up_back)


def plain_body(inputs, out_grad, w_gate, w_up, w_down):
    gathered_in = lax.all_gather(inputs, "gx", axis=0, tiled=True)
    gathered_grad = lax.all_gather(out_grad, "gx", axis=0, tiled=True)
    parts = (dot(gathered_in, w_gate, NN), dot(gathered_in, w_up, NN), dot(gathered_grad, w_down, NT))
    hidden, gate_back, up_back = swiglu_back(*lax.psum(parts, "gy"))
    down_wgrad = dot(hidden, gathered_grad, TN).astype(BF)
    gate_wgrad = dot(gathered_in, gate_back, TN).astype(BF)
    up_wgrad = dot(gathered_in, up_back, TN).astype(BF)
    result = dot(gate_back, w_gate, NT) + dot(up_back, w_up, NT)
    summed = lax.psum_scatter(result, "gx", scatter_dimension=0, tiled=True)
    return (summed.astype(BF), gate_wgrad, up_wgrad, down_wgrad)


def solution(mesh):
    n = mesh.shape["gx"]

    def body(inputs, out_grad, w_gate, w_up, w_down):
        args = (inputs, out_grad, w_gate, w_up, w_down)
        if n % 4 == 0 and n >= 8 and mesh.shape["gy"] == 2 and inputs.shape[0] % 16 == 0:
            return ring_body(n, *args)
        return plain_body(*args)

    in_specs = (
        P(("groups", "gx"), "gy"),
        P(("groups", "gx"), "gy"),
        P("gy", "gx"),
        P("gy", "gx"),
        P("gx", "gy"),
    )
    out_specs = (
        P(("groups", "gx"), "gy"),
        P(("groups", "gy"), "gx"),
        P(("groups", "gy"), "gx"),
        P(("groups", "gx"), "gy"),
    )
    return jax.shard_map(body, mesh=mesh, in_specs=in_specs, out_specs=out_specs, check_vma=False)
```

time: 422 us -> 194 us (0.46)
  waiting for transfers between devices: 237 us -> 45.9 us
  matrix products: 126 us -> 0 us
  Pallas kernels: 0 us -> 118 us
  local copies, waits for them, and re-layouts: 37.4 us -> 6.09 us
  starting transfers between devices: 0.34 us -> 21 us
  between operations: 13.8 us -> 0.94 us
  other arithmetic: 7.17 us -> 1.49 us
    dot_general x8 -> x0, matrix products: 126 us -> none  [the longest x1 26.5 us: body(): lax.dot_general(up_back, w_up, contract_last, preferred_element_type=jnp....]
    all_gather x2 -> x0, waiting for transfers between devices: 122 us -> none  [the longest x1 77.6 us: body(): lax.all_gather(inputs, 'gx', axis=0, tiled=True)]
    pallas_call x0 -> x11, Pallas kernels: none -> 118 us  [the longest x2 39.3 us: backward(): call(kernel, name, 4 * tokens * depth * width, 20 * tokens * width, 31, g...]
    reduce_scatter x1 -> x0, waiting for transfers between devices: 71.3 us -> none  [body(): lax.psum_scatter(result + lax.dot_general(up_back, w_up, contract_last, p...]
    ppermute x0 -> x25, waiting for transfers between devices: none -> 45.9 us  [the longest x11 23 us: swap(): return lax.ppermute(x, 'gx', across)]
    psum x1 -> x0, waiting for transfers between devices: 42.1 us -> none  [body(): lax.psum((gate_part, up_part, back_part), 'gy')]
    unnamed x6 -> x46, local copies, waits for them, and re-layouts: 37.4 us -> 6.09 us
    ppermute x0 -> x25, starting transfers between devices: none -> 21 us  [the longest x11 13.6 us: swap(): return lax.ppermute(x, 'gx', across)]
  transfers between devices with their start and end apart: 4 -> 25, of which waited for: 4 -> 14; matrix products, arithmetic and copies ran while one was open for 26% -> 0% of each run, Pallas kernels for 0% -> 61%
where the time goes in v2:
time: 194 us
  Pallas kernels  118 us (61%)
  waiting for transfers between devices  45.9 us (24%)
  starting transfers between devices  21 us (11%)
  local copies, waits for them, and re-layouts  6.09 us (3%)
    pallas_call x2, Pallas kernels, backward(): call(kernel, name, 4 * tokens * depth * width, 20 * tokens * width, 31, g...  39.3 us
    pallas_call x4, Pallas kernels, gather_matmul(): call(kernel, name, 2 * tokens * depth * width * nw, 2 * tokens * depth, 1...  33.1 us
    pallas_call x2, Pallas kernels, weight_grads(): call(kernel, name, 2 * tokens * depth * width * count, 2 * depth * width...  30.4 us
    ppermute x11, waiting for transfers between devices, swap(): return lax.ppermute(x, 'gx', across)  23 us
    ppermute x10, waiting for transfers between devices, shift(): return lax.ppermute(x, 'gx', pairs)  22.4 us
    pallas_call x3, Pallas kernels, hold(): call(kernel, name, 0, 2 * weight.size, vmem, in_specs=[HBM_SPEC], out_spe...  15.5 us
    ppermute x11, starting transfers between devices, swap(): return lax.ppermute(x, 'gx', across)  13.6 us
    ppermute x10, starting transfers between devices, shift(): return lax.ppermute(x, 'gx', pairs)  6.29 us
  transfers between devices with their start and end apart: 25, of which 14 were waited for; matrix products, arithmetic and copies ran while one was open for 0% of the time, Pallas kernels for 61%

profile of v2, /device:TPU:0, one launch (start us, length us, event | category | flops | bytes accessed | tf_op | source)
XLA Modules:
  0.0 193.8 jit_solution(15671702250962273208)
XLA Ops:
  0.6 3.1 %collective-permute-start = (bf16[64,4096]{1,0:T(8,128)(2,1)}, bf16[64,4096]{1,0:T(8,128)(2,1)S(1)}, u32[]{:S(2)}, u32[]{:S(2)}) collective-permute-start(bf16[64,4096]{1,0:T(8,128)(2,1)} %refs_2_), channel_id=1, source_target_pairs={{0,4},{2,6},{4,8},{6,10},{8,12},{10,14},{12,0},{14,2},{1,5},{3,7},... | collective-permute-start | bytes 1572872 | tf_op jit(solution)/shard_map/ppermute | solution.py:234
  3.7 1.5 collective-permute-start.1
  5.2 5.2 %hold_gate.1.refs_4_ = bf16[4096,1792]{1,0:T(8,128)(2,1)S(1)} custom-call(bf16[4096,1792]{1,0:T(8,128)(2,1)} %w_ref.1), custom_call_target="tpu_custom_call" | custom-call | bytes 14680064 | tf_op jit(solution)/shard_map/hold_gate/pallas_call | solution.py:54
  10.4 7.4 %collective-permute-done.refs_0_ = bf16[64,4096]{1,0:T(8,128)(2,1)S(1)} collective-permute-done((bf16[64,4096]{1,0:T(8,128)(2,1)}, bf16[64,4096]{1,0:T(8,128)(2,1)S(1)}, u32[]{:S(2)}, u32[]{:S(2)}) %collective-permute-start) | collective-permute-done | bytes 524320 | tf_op jit(solution)/shard_map/ppermute | solution.py:234
  17.9 1.5 collective-permute-start.3
  20.4 5.2 %hold_up.1.refs_5_ = bf16[4096,1792]{1,0:T(8,128)(2,1)S(1)} custom-call(bf16[4096,1792]{1,0:T(8,128)(2,1)} %w_ref.2), custom_call_target="tpu_custom_call" | custom-call | bytes 14680064 | tf_op jit(solution)/shard_map/hold_up/pallas_call | solution.py:54
  25.6 5.4 %collective-permute-done.3.refs_1_ = bf16[64,4096]{1,0:T(8,128)(2,1)S(1)} collective-permute-done((bf16[64,4096]{1,0:T(8,128)(2,1)S(1)}, bf16[64,4096]{1,0:T(8,128)(2,1)S(1)}, u32[]{:S(2)}, u32[]{:S(2)}) %collective-permute-start.3) | collective-permute-done | bytes 524320 | tf_op jit(solution)/shard_map/ppermute | solution.py:237
  31.0 2.8 %collective-permute-done.2.refs_2_ = bf16[64,4096]{1,0:T(8,128)(2,1)S(1)} collective-permute-done((bf16[64,4096]{1,0:T(8,128)(2,1)S(1)}, bf16[64,4096]{1,0:T(8,128)(2,1)S(1)}, u32[]{:S(2)}, u32[]{:S(2)}) %collective-permute-start.2) | collective-permute-done | bytes 524320 | tf_op jit(solution)/shard_map/ppermute | solution.py:234
  34.5 10.9 %collective-permute-done.5.refs_3_ = bf16[64,4096]{1,0:T(8,128)(2,1)S(1)} collective-permute-done((bf16[64,4096]{1,0:T(8,128)(2,1)S(1)}, bf16[64,4096]{1,0:T(8,128)(2,1)S(1)}, u32[]{:S(2)}, u32[]{:S(2)}) %collective-permute-start.5) | collective-permute-done | bytes 524320 | tf_op jit(solution)/shard_map/ppermute | solution.py:237
  45.4 2.5 %collective-permute-done.4.refs_0_ = bf16[64,4096]{1,0:T(8,128)(2,1)S(1)} collective-permute-done((bf16[64,4096]{1,0:T(8,128)(2,1)S(1)}, bf16[64,4096]{1,0:T(8,128)(2,1)S(1)}, u32[]{:S(2)}, u32[]{:S(2)}) %collective-permute-start.4) | collective-permute-done | bytes 524320 | tf_op jit(solution)/shard_map/ppermute | solution.py:234
  49.0 10.1 %gu_a.1 = (bf16[256,4096]{1,0:T(8,128)(2,1)}, f32[2,256,1792]{2,1,0:T(8,128)}, bf16[2,256,1792]{2,1,0:T(8,128)(2,1)}) custom-call(bf16[64,4096]{1,0:T(8,128)(2,1)S(1)} %collective-permute-done.refs_0_, bf16[64,4096]{1,0:T(8,128)(2,1)S(1)} %collective-permute-done.3.refs_1_, bf16[64,4096]{1,0:T(8,128)(2,1)S(1)} %collective-permute-done.2.refs_2_, ...), custom_call_target="tpu_custom_call" | custom-call | flops 7516192768 | bytes 2097152 | tf_op jit(solution)/shard_map/gu_a/pallas_call | solution.py:95
  59.1 1.3 collective-permute-done.6.refs_0_
  61.3 10.2 %gu_b.1 = (bf16[256,4096]{1,0:T(8,128)(2,1)}, f32[2,256,1792]{2,1,0:T(8,128)}, bf16[2,256,1792]{2,1,0:T(8,128)(2,1)}) custom-call(bf16[64,4096]{1,0:T(8,128)(2,1)S(1)} %collective-permute-done.4.refs_0_, bf16[64,4096]{1,0:T(8,128)(2,1)S(1)} %collective-permute-done.7.refs_1_, bf16[64,4096]{1,0:T(8,128)(2,1)S(1)} %copy-done.5, ...), custom_call_target="tpu_custom_call" | custom-call | flops 7516192768 | bytes 2097152 | tf_op jit(solution)/shard_map/gu_b/pallas_call | solution.py:95
  72.3 2.1 %collective-permute-start.11 = (bf16[64,4096]{1,0:T(8,128)(2,1)S(1)}, bf16[64,4096]{1,0:T(8,128)(2,1)S(1)}, u32[]{:S(2)}, u32[]{:S(2)}) collective-permute-start(bf16[64,4096]{1,0:T(8,128)(2,1)S(1)} %collective-permute-done.8.refs_2_), channel_id=1, source_target_pairs={{0,2},{2,0},{4,6},{6,4},{8,10},{10,8},{12,14},{14,12},{1,3},{3,1},... | collective-permute-start | bytes 1572872 | tf_op jit(solution)/shard_map/ppermute | solution.py:237
  74.4 5.2 %hold_down.1.refs_4_ = bf16[1792,4096]{1,0:T(8,128)(2,1)S(1)} custom-call(bf16[1792,4096]{1,0:T(8,128)(2,1)} %w_ref.3), custom_call_target="tpu_custom_call" | custom-call | bytes 14680064 | tf_op jit(solution)/shard_map/hold_down/pallas_call | solution.py:54
  79.6 3.2 %collective-permute-done.11.refs_3_ = bf16[64,4096]{1,0:T(8,128)(2,1)S(1)} collective-permute-done((bf16[64,4096]{1,0:T(8,128)(2,1)S(1)}, bf16[64,4096]{1,0:T(8,128)(2,1)S(1)}, u32[]{:S(2)}, u32[]{:S(2)}) %collective-permute-start.11) | collective-permute-done | bytes 524320 | tf_op jit(solution)/shard_map/ppermute | solution.py:237
  82.8 4.6 %collective-permute-done.10.refs_0_ = bf16[64,4096]{1,0:T(8,128)(2,1)S(1)} collective-permute-done((bf16[64,4096]{1,0:T(8,128)(2,1)S(1)}, bf16[64,4096]{1,0:T(8,128)(2,1)S(1)}, u32[]{:S(2)}, u32[]{:S(2)}) %collective-permute-start.10) | collective-permute-done | bytes 524320 | tf_op jit(solution)/shard_map/ppermute | solution.py:234
  87.3 6.4 %h_a.1 = (bf16[256,4096]{1,0:T(8,128)(2,1)}, f32[1,256,1792]{2,1,0:T(8,128)}, bf16[1,256,1792]{2,1,0:T(8,128)(2,1)}) custom-call(bf16[64,4096]{1,0:T(8,128)(2,1)S(1)} %collective-permute-done.6.refs_0_, bf16[64,4096]{1,0:T(8,128)(2,1)S(1)} %collective-permute-done.9.refs_1_, bf16[64,4096]{1,0:T(8,128)(2,1)S(1)} %collective-permute-done.8.refs_2_, ...), custom_call_target="tpu_custom_call" | custom-call | flops 3758096384 | bytes 2097152 | tf_op jit(solution)/shard_map/h_a/pallas_call | solution.py:95
  93.8 2.7 %collective-permute-done.13.refs_3_ = bf16[64,4096]{1,0:T(8,128)(2,1)S(1)} collective-permute-done((bf16[64,4096]{1,0:T(8,128)(2,1)S(1)}, bf16[64,4096]{1,0:T(8,128)(2,1)S(1)}, u32[]{:S(2)}, u32[]{:S(2)}) %collective-permute-start.13) | collective-permute-done | bytes 524320 | tf_op jit(solution)/shard_map/ppermute | solution.py:237
  96.5 1.8 collective-permute-done.12.refs_1_
  98.8 6.4 %h_b.1 = (bf16[256,4096]{1,0:T(8,128)(2,1)}, f32[1,256,1792]{2,1,0:T(8,128)}, bf16[1,256,1792]{2,1,0:T(8,128)(2,1)}) custom-call(bf16[64,4096]{1,0:T(8,128)(2,1)S(1)} %collective-permute-done.10.refs_0_, bf16[64,4096]{1,0:T(8,128)(2,1)S(1)} %collective-permute-done.12.refs_1_, bf16[64,4096]{1,0:T(8,128)(2,1)S(1)} %copy-done.6, ...), custom_call_target="tpu_custom_call" | custom-call | flops 3758096384 | bytes 2097152 | tf_op jit(solution)/shard_map/h_b/pallas_call | solution.py:95
  107.2 1.2 copy-done.1
  108.4 1.5 copy-done.2
  109.9 1.2 copy-done.4
  111.1 19.7 %back_a.1 = (bf16[64,4096]{1,0:T(8,128)(2,1)}, bf16[64,4096]{1,0:T(8,128)(2,1)}, bf16[64,4096]{1,0:T(8,128)(2,1)}, bf16[64,4096]{1,0:T(8,128)(2,1)}, bf16[256,17...) custom-call(f32[2,256,1792]{2,1,0:T(8,128)} %get-tuple-element.216.refs_0_, ...), custom_call_target="tpu_custom_call" | custom-call | flops 7516192768 | bytes 9175040 | tf_op jit(solution)/shard_map/back_a/pallas_call | solution.py:157
  130.8 2.1 %collective-permute-start.16 = (bf16[64,4096]{1,0:T(8,128)(2,1)}, bf16[64,4096]{1,0:T(8,128)(2,1)S(1)}, u32[]{:S(2)}, u32[]{:S(2)}) collective-permute-start(bf16[64,4096]{1,0:T(8,128)(2,1)} %get-tuple-element.239), channel_id=1, source_target_pairs={{0,2},{2,0},{4,6},{6,4},{8,10},{10,8},{12,14},{14,12},{1,3},{3,1},... | collective-permute-start | bytes 1572872 | tf_op jit(solution)/shard_map/ppermute | solution.py:237
  133.0 19.7 %back_b.1 = (bf16[64,4096]{1,0:T(8,128)(2,1)}, bf16[64,4096]{1,0:T(8,128)(2,1)}, bf16[64,4096]{1,0:T(8,128)(2,1)}, bf16[64,4096]{1,0:T(8,128)(2,1)}, bf16[256,17...) custom-call(f32[2,256,1792]{2,1,0:T(8,128)} %get-tuple-element.240.refs_0_, ...), custom_call_target="tpu_custom_call" | custom-call | flops 7516192768 | bytes 9175040 | tf_op jit(solution)/shard_map/back_b/pallas_call | solution.py:157
  152.9 2.0 %collective-permute-start.21 = (bf16[64,4096]{1,0:T(8,128)(2,1)}, bf16[64,4096]{1,0:T(8,128)(2,1)S(1)}, u32[]{:S(2)}, u32[]{:S(2)}) collective-permute-start(bf16[64,4096]{1,0:T(8,128)(2,1)} %get-tuple-element.255), channel_id=1, source_target_pairs={{0,2},{2,0},{4,6},{6,4},{8,10},{10,8},{12,14},{14,12},{1,3},{3,1},... | collective-permute-start | bytes 1572872 | tf_op jit(solution)/shard_map/ppermute | solution.py:237
  156.1 10.8 %down_wgrad.1 = bf16[1792,4096]{1,0:T(8,128)(2,1)} custom-call(bf16[256,1792]{1,0:T(8,128)(2,1)S(1)} %copy-done.15, bf16[256,1792]{1,0:T(8,128)(2,1)S(1)} %copy-done.16, bf16[256,4096]{1,0:T(8,128)(2,1)S(1)} %copy-done.9, bf16[256,4096]{1,0:T(8,128)(2,1)S(1)} %copy-done.10), custom_call_target="tpu_custom_call" | custom-call | flops 7516192768 | bytes 14680064 | tf_op jit(solution)/shard_map/down_wgrad/pallas_call | solution.py:199
  168.9 1.7 collective-permute-start.22
  170.7 1.2 collective-permute-start.24
  172.0 19.5 %in_wgrads.1 = (bf16[4096,1792]{1,0:T(8,128)(2,1)}, bf16[4096,1792]{1,0:T(8,128)(2,1)}) custom-call(bf16[256,4096]{1,0:T(8,128)(2,1)S(1)} %copy-done.7, bf16[256,4096]{1,0:T(8,128)(2,1)S(1)} %copy-done.8, bf16[256,1792]{1,0:T(8,128)(2,1)S(1)} %copy-done.11, bf16[256,1792]{1,0:T(8,128)(2,1)S(1)} %copy-done.13, bf16[256,1792]{1,0:T(8,128)(2,1)S(1)} %copy-done.12, ...), custom_call_target="tpu_custom_call" | custom-call | flops 15032385536 | bytes 29360128 | tf_op jit(solution)/shard_map/in_wgrads/pallas_call | solution.py:199
  (79 shorter events, 12.7 us)
Async XLA Ops:
  0.6 17.2 %collective-permute-start = (bf16[64,4096]{1,0:T(8,128)(2,1)}, bf16[64,4096]{1,0:T(8,128)(2,1)S(1)}, u32[]{:S(2)}, u32[]{:S(2)}) collective-permute-start(bf16[64,4096]{1,0:T(8,128)(2,1)} %refs_2_), channel_id=1, source_target_pairs={{0,4},{2,6},{4,8},{6,10},{8,12},{10,14},{12,0},{14,2},{1,5},{3,7},... | collective-permute-start | bytes 1572872 | tf_op jit(solution)/shard_map/ppermute | solution.py:234
  3.7 14.2 %collective-permute-start.1 = (bf16[64,4096]{1,0:T(8,128)(2,1)}, bf16[64,4096]{1,0:T(8,128)(2,1)S(1)}, u32[]{:S(2)}, u32[]{:S(2)}) collective-permute-start(bf16[64,4096]{1,0:T(8,128)(2,1)} %refs_2_), channel_id=1, source_target_pairs={{0,2},{2,0},{4,6},{6,4},{8,10},{10,8},{12,14},{14,12},{1,3},{3,1},... | collective-permute-start | bytes 1572872 | tf_op jit(solution)/shard_map/ppermute | solution.py:237
  10.4 37.5 %copy-start.6 = (bf16[64,4096]{1,0:T(8,128)(2,1)S(1)}, bf16[64,4096]{1,0:T(8,128)(2,1)}, u32[]{:S(2)}) copy-start(bf16[64,4096]{1,0:T(8,128)(2,1)} %refs_2_.1) | copy-start | bytes 1572868
  17.9 13.1 %collective-permute-start.3 = (bf16[64,4096]{1,0:T(8,128)(2,1)S(1)}, bf16[64,4096]{1,0:T(8,128)(2,1)S(1)}, u32[]{:S(2)}, u32[]{:S(2)}) collective-permute-start(bf16[64,4096]{1,0:T(8,128)(2,1)S(1)} %collective-permute-done.refs_0_), channel_id=1, source_target_pairs={{0,2},{2,0},{4,6},{6,4},{8,10},{10,8},{12,14},{14,12},{1,3},{3,1},... | collective-permute-start | bytes 1572872 | tf_op jit(solution)/shard_map/ppermute | solution.py:237
  19.4 14.4 %collective-permute-start.2 = (bf16[64,4096]{1,0:T(8,128)(2,1)S(1)}, bf16[64,4096]{1,0:T(8,128)(2,1)S(1)}, u32[]{:S(2)}, u32[]{:S(2)}) collective-permute-start(bf16[64,4096]{1,0:T(8,128)(2,1)S(1)} %collective-permute-done.refs_0_), channel_id=1, source_target_pairs={{0,4},{2,6},{4,8},{6,10},{8,12},{10,14},{12,0},{14,2},{1,5},{3,7},... | collective-permute-start | bytes 1572872 | tf_op jit(solution)/shard_map/ppermute | solution.py:234
  25.6 35.7 %copy-start = (bf16[4096,1792]{1,0:T(8,128)(2,1)}, bf16[4096,1792]{1,0:T(8,128)(2,1)S(1)}, u32[]{:S(2)}) copy-start(bf16[4096,1792]{1,0:T(8,128)(2,1)S(1)} %hold_up.1.refs_5_) | copy-start | bytes 44040196
  25.6 35.7 %copy-start.5 = (bf16[64,4096]{1,0:T(8,128)(2,1)S(1)}, bf16[64,4096]{1,0:T(8,128)(2,1)}, u32[]{:S(2)}) copy-start(bf16[64,4096]{1,0:T(8,128)(2,1)} %refs_2_) | copy-start | bytes 1572868
  33.8 11.7 %collective-permute-start.5 = (bf16[64,4096]{1,0:T(8,128)(2,1)S(1)}, bf16[64,4096]{1,0:T(8,128)(2,1)S(1)}, u32[]{:S(2)}, u32[]{:S(2)}) collective-permute-start(bf16[64,4096]{1,0:T(8,128)(2,1)S(1)} %collective-permute-done.2.refs_2_), channel_id=1, source_target_pairs={{0,2},{2,0},{4,6},{6,4},{8,10},{10,8},{12,14},{14,12},{1,3},{3,1},... | collective-permute-start | bytes 1572872 | tf_op jit(solution)/shard_map/ppermute | solution.py:237
  34.5 13.4 %collective-permute-start.4 = (bf16[64,4096]{1,0:T(8,128)(2,1)S(1)}, bf16[64,4096]{1,0:T(8,128)(2,1)S(1)}, u32[]{:S(2)}, u32[]{:S(2)}) collective-permute-start(bf16[64,4096]{1,0:T(8,128)(2,1)S(1)} %collective-permute-done.2.refs_2_), channel_id=1, source_target_pairs={{0,4},{2,6},{4,8},{6,10},{8,12},{10,14},{12,0},{14,2},{1,5},{3,7},... | collective-permute-start | bytes 1572872 | tf_op jit(solution)/shard_map/ppermute | solution.py:234
  48.0 12.5 %collective-permute-start.6 = (bf16[64,4096]{1,0:T(8,128)(2,1)S(1)}, bf16[64,4096]{1,0:T(8,128)(2,1)S(1)}, u32[]{:S(2)}, u32[]{:S(2)}) collective-permute-start(bf16[64,4096]{1,0:T(8,128)(2,1)S(1)} %copy-done.6), channel_id=1, source_target_pairs={{0,4},{2,6},{4,8},{6,10},{8,12},{10,14},{12,0},{14,2},{1,5},{3,7},... | collective-permute-start | bytes 1572872 | tf_op jit(solution)/shard_map/ppermute | solution.py:234
  48.0 12.5 %collective-permute-start.7 = (bf16[64,4096]{1,0:T(8,128)(2,1)S(1)}, bf16[64,4096]{1,0:T(8,128)(2,1)S(1)}, u32[]{:S(2)}, u32[]{:S(2)}) collective-permute-start(bf16[64,4096]{1,0:T(8,128)(2,1)S(1)} %collective-permute-done.4.refs_0_), channel_id=1, source_target_pairs={{0,2},{2,0},{4,6},{6,4},{8,10},{10,8},{12,14},{14,12},{1,3},{3,1},... | collective-permute-start | bytes 1572872 | tf_op jit(solution)/shard_map/ppermute | solution.py:237
  60.5 11.0 %collective-permute-start.9 = (bf16[64,4096]{1,0:T(8,128)(2,1)S(1)}, bf16[64,4096]{1,0:T(8,128)(2,1)S(1)}, u32[]{:S(2)}, u32[]{:S(2)}) collective-permute-start(bf16[64,4096]{1,0:T(8,128)(2,1)S(1)} %collective-permute-done.6.refs_0_), channel_id=1, source_target_pairs={{0,2},{2,0},{4,6},{6,4},{8,10},{10,8},{12,14},{14,12},{1,3},{3,1},... | collective-permute-start | bytes 1572872 | tf_op jit(solution)/shard_map/ppermute | solution.py:237
  61.3 11.1 %collective-permute-start.8 = (bf16[64,4096]{1,0:T(8,128)(2,1)S(1)}, bf16[64,4096]{1,0:T(8,128)(2,1)S(1)}, u32[]{:S(2)}, u32[]{:S(2)}) collective-permute-start(bf16[64,4096]{1,0:T(8,128)(2,1)S(1)} %collective-permute-done.6.refs_0_), channel_id=1, source_target_pairs={{0,4},{2,6},{4,8},{6,10},{8,12},{10,14},{12,0},{14,2},{1,5},{3,7},... | collective-permute-start | bytes 1572872 | tf_op jit(solution)/shard_map/ppermute | solution.py:234
  72.3 10.4 %collective-permute-start.11 = (bf16[64,4096]{1,0:T(8,128)(2,1)S(1)}, bf16[64,4096]{1,0:T(8,128)(2,1)S(1)}, u32[]{:S(2)}, u32[]{:S(2)}) collective-permute-start(bf16[64,4096]{1,0:T(8,128)(2,1)S(1)} %collective-permute-done.8.refs_2_), channel_id=1, source_target_pairs={{0,2},{2,0},{4,6},{6,4},{8,10},{10,8},{12,14},{14,12},{1,3},{3,1},... | collective-permute-start | bytes 1572872 | tf_op jit(solution)/shard_map/ppermute | solution.py:237
  74.4 12.9 %collective-permute-start.10 = (bf16[64,4096]{1,0:T(8,128)(2,1)S(1)}, bf16[64,4096]{1,0:T(8,128)(2,1)S(1)}, u32[]{:S(2)}, u32[]{:S(2)}) collective-permute-start(bf16[64,4096]{1,0:T(8,128)(2,1)S(1)} %collective-permute-done.8.refs_2_), channel_id=1, source_target_pairs={{0,4},{2,6},{4,8},{6,10},{8,12},{10,14},{12,0},{14,2},{1,5},{3,7},... | collective-permute-start | bytes 1572872 | tf_op jit(solution)/shard_map/ppermute | solution.py:234
  87.3 9.2 %collective-permute-start.13 = (bf16[64,4096]{1,0:T(8,128)(2,1)S(1)}, bf16[64,4096]{1,0:T(8,128)(2,1)S(1)}, u32[]{:S(2)}, u32[]{:S(2)}) collective-permute-start(bf16[64,4096]{1,0:T(8,128)(2,1)S(1)} %copy-done.6), channel_id=1, source_target_pairs={{0,2},{2,0},{4,6},{6,4},{8,10},{10,8},{12,14},{14,12},{1,3},{3,1},... | collective-permute-start | bytes 1572872 | tf_op jit(solution)/shard_map/ppermute | solution.py:237
  87.3 11.0 %collective-permute-start.12 = (bf16[64,4096]{1,0:T(8,128)(2,1)S(1)}, bf16[64,4096]{1,0:T(8,128)(2,1)S(1)}, u32[]{:S(2)}, u32[]{:S(2)}) collective-permute-start(bf16[64,4096]{1,0:T(8,128)(2,1)S(1)} %collective-permute-done.11.refs_3_), channel_id=1, source_target_pairs={{0,4},{2,6},{4,8},{6,10},{8,12},{10,14},{12,0},{14,2},{1,5},{3,7},... | collective-permute-start | bytes 1572872 | tf_op jit(solution)/shard_map/ppermute | solution.py:234
  98.3 8.9 %collective-permute-start.14 = (bf16[2,256,1792]{2,1,0:T(8,128)(2,1)S(1)}, bf16[2,256,1792]{2,1,0:T(8,128)(2,1)S(1)}, u32[]{:S(2)}, u32[]{:S(2)}) collective-permute-start(bf16[2,256,1792]{2,1,0:T(8,128)(2,1)S(1)} %copy-done.21), channel_id=1, source_target_pairs={{0,1},{1,0},{2,3},{3,2},{4,5},{5,4},{6,7},{7,6},{8,9},{9,8},{10,11... | collective-permute-start | bytes 5505032 | tf_op jit(solution)/shard_map/ppermute | solution.py:240
  98.3 34.6 %collective-permute-start.17 = (bf16[2,256,1792]{2,1,0:T(8,128)(2,1)}, bf16[2,256,1792]{2,1,0:T(8,128)(2,1)S(1)}, u32[]{:S(2)}, u32[]{:S(2)}) collective-permute-start(bf16[2,256,1792]{2,1,0:T(8,128)(2,1)} %get-tuple-element.241), channel_id=1, source_target_pairs={{0,1},{1,0},{2,3},{3,2},{4,5},{5,4},{6,7},{7,6},{8,9},{9,8},{10,11... | collective-permute-start | bytes 5505032 | tf_op jit(solution)/shard_map/ppermute | solution.py:240
  98.8 7.4 %collective-permute-start.15 = (bf16[1,256,1792]{2,1,0:T(8,128)(2,1)}, bf16[1,256,1792]{2,1,0:T(8,128)(2,1)S(1)}, u32[]{:S(2)}, u32[]{:S(2)}) collective-permute-start(bf16[1,256,1792]{2,1,0:T(8,128)(2,1)} %get-tuple-element.228), channel_id=1, source_target_pairs={{0,1},{1,0},{2,3},{3,2},{4,5},{5,4},{6,7},{7,6},{8,9},{9,8},{10,11... | collective-permute-start | bytes 2752520 | tf_op jit(solution)/shard_map/ppermute | solution.py:240
  105.2 27.7 %collective-permute-start.18 = (bf16[1,256,1792]{2,1,0:T(8,128)(2,1)}, bf16[1,256,1792]{2,1,0:T(8,128)(2,1)S(1)}, u32[]{:S(2)}, u32[]{:S(2)}) collective-permute-start(bf16[1,256,1792]{2,1,0:T(8,128)(2,1)} %get-tuple-element.243), channel_id=1, source_target_pairs={{0,1},{1,0},{2,3},{3,2},{4,5},{5,4},{6,7},{7,6},{8,9},{9,8},{10,11... | collective-permute-start | bytes 2752520 | tf_op jit(solution)/shard_map/ppermute | solution.py:240
  130.7 24.1 %copy-start.9 = (bf16[256,4096]{1,0:T(8,128)(2,1)S(1)}, bf16[256,4096]{1,0:T(8,128)(2,1)}, u32[]{:S(2)}) copy-start(bf16[256,4096]{1,0:T(8,128)(2,1)} %get-tuple-element.259.refs_2_) | copy-start | bytes 6291460
  130.8 24.1 %copy-start.10 = (bf16[256,4096]{1,0:T(8,128)(2,1)S(1)}, bf16[256,4096]{1,0:T(8,128)(2,1)}, u32[]{:S(2)}) copy-start(bf16[256,4096]{1,0:T(8,128)(2,1)} %get-tuple-element.260.refs_3_) | copy-start | bytes 6291460
  130.8 24.1 %copy-start.15 = (bf16[256,1792]{1,0:T(8,128)(2,1)S(1)}, bf16[256,1792]{1,0:T(8,128)(2,1)}, u32[]{:S(2)}) copy-start(bf16[256,1792]{1,0:T(8,128)(2,1)} %get-tuple-element.257.refs_0_) | copy-start | bytes 2752516
  130.8 21.8 %collective-permute-start.16 = (bf16[64,4096]{1,0:T(8,128)(2,1)}, bf16[64,4096]{1,0:T(8,128)(2,1)S(1)}, u32[]{:S(2)}, u32[]{:S(2)}) collective-permute-start(bf16[64,4096]{1,0:T(8,128)(2,1)} %get-tuple-element.239), channel_id=1, source_target_pairs={{0,2},{2,0},{4,6},{6,4},{8,10},{10,8},{12,14},{14,12},{1,3},{3,1},... | collective-permute-start | bytes 1572872 | tf_op jit(solution)/shard_map/ppermute | solution.py:237
  132.9 34.1 %collective-permute-start.20 = (bf16[64,4096]{1,0:T(8,128)(2,1)}, bf16[64,4096]{1,0:T(8,128)(2,1)S(1)}, u32[]{:S(2)}, u32[]{:S(2)}) collective-permute-start(bf16[64,4096]{1,0:T(8,128)(2,1)} %get-tuple-element.254), channel_id=1, source_target_pairs={{0,2},{2,0},{4,6},{6,4},{8,10},{10,8},{12,14},{14,12},{1,3},{3,1},... | collective-permute-start | bytes 1572872 | tf_op jit(solution)/shard_map/ppermute | solution.py:237
  152.8 14.1 %collective-permute-start.19 = (bf16[64,4096]{1,0:T(8,128)(2,1)S(1)}, bf16[64,4096]{1,0:T(8,128)(2,1)S(1)}, u32[]{:S(2)}, u32[]{:S(2)}) collective-permute-start(bf16[64,4096]{1,0:T(8,128)(2,1)S(1)} %add_convert_fusion.3), channel_id=1, source_target_pairs={{0,12},{2,14},{4,0},{6,2},{8,4},{10,6},{12,8},{14,10},{1,13},{3,15... | collective-permute-start | bytes 1572872 | tf_op jit(solution)/shard_map/ppermute | solution.py:234
  152.9 14.9 %collective-permute-start.21 = (bf16[64,4096]{1,0:T(8,128)(2,1)}, bf16[64,4096]{1,0:T(8,128)(2,1)S(1)}, u32[]{:S(2)}, u32[]{:S(2)}) collective-permute-start(bf16[64,4096]{1,0:T(8,128)(2,1)} %get-tuple-element.255), channel_id=1, source_target_pairs={{0,2},{2,0},{4,6},{6,4},{8,10},{10,8},{12,14},{14,12},{1,3},{3,1},... | collective-permute-start | bytes 1572872 | tf_op jit(solution)/shard_map/ppermute | solution.py:237
  168.0 24.7 %collective-permute-start.23 = (bf16[64,4096]{1,0:T(8,128)(2,1)S(1)}, bf16[64,4096]{1,0:T(8,128)(2,1)S(1)}, u32[]{:S(2)}, u32[]{:S(2)}) collective-permute-start(bf16[64,4096]{1,0:T(8,128)(2,1)S(1)} %add_convert_fusion.2), channel_id=1, source_target_pairs={{0,12},{2,14},{4,0},{6,2},{8,4},{10,6},{12,8},{14,10},{1,13},{3,15... | collective-permute-start | bytes 1572872 | tf_op jit(solution)/shard_map/ppermute | solution.py:234
  168.9 23.8 %collective-permute-start.22 = (bf16[64,4096]{1,0:T(8,128)(2,1)S(1)}, bf16[64,4096]{1,0:T(8,128)(2,1)S(1)}, u32[]{:S(2)}, u32[]{:S(2)}) collective-permute-start(bf16[64,4096]{1,0:T(8,128)(2,1)S(1)} %copy-done.22), channel_id=1, source_target_pairs={{0,2},{2,0},{4,6},{6,4},{8,10},{10,8},{12,14},{14,12},{1,3},{3,1},... | collective-permute-start | bytes 1572872 | tf_op jit(solution)/shard_map/ppermute | solution.py:237
  170.7 22.0 %copy-start.17 = (bf16[64,4096]{1,0:T(8,128)(2,1)S(1)}, bf16[64,4096]{1,0:T(8,128)(2,1)}, u32[]{:S(2)}) copy-start(bf16[64,4096]{1,0:T(8,128)(2,1)} %get-tuple-element.251) | copy-start | bytes 1572868
  170.7 22.0 %collective-permute-start.24 = (bf16[64,4096]{1,0:T(8,128)(2,1)S(1)}, bf16[64,4096]{1,0:T(8,128)(2,1)S(1)}, u32[]{:S(2)}, u32[]{:S(2)}) collective-permute-start(bf16[64,4096]{1,0:T(8,128)(2,1)S(1)} %add_convert_fusion.1), channel_id=1, source_target_pairs={{0,4},{2,6},{4,8},{6,10},{8,12},{10,14},{12,0},{14,2},{1,5},{3,7},... | collective-permute-start | bytes 1572872 | tf_op jit(solution)/shard_map/ppermute | solution.py:234
  (16 other events, 169.8 us)

commit v3 on v2

--- a/solution.py
+++ b/solution.py
@@ -54,8 +54,8 @@
     return call(
         kernel,
         name,
-        0,
-        2 * weight.size,
+        1500 * weight.size,
+        4 * weight.size,
         vmem,
         in_specs=[HBM_SPEC],
         out_specs=VMEM_SPEC,
@@ -214,18 +214,18 @@
     return lax.optimization_barrier(arrays)
 
 
-def gather_stages(ring):
-    along = [f"in {k}" for k in range(1, ring)] + [f"grad {k}" for k in range(1, ring)] + [f"grad other {ring - 1}"]
-    across = [f"in other {k}" for k in range(ring)] + [f"grad other {k}" for k in range(1, ring - 1)] + ["grad other 0"]
-    kernels = [["gate"], ["up"]] + [[]] * (ring - 3) + [["a"], ["b"], ["down"]]
-    kernels += [[]] * (len(along) - 1 - len(kernels)) + [["h_a"]]
-    return [([m, s], k) for m, s, k in zip(along, across, kernels)]
+STAGES = [
+    (["in 1", "in other 0", "in 3", "grad other 0"], ["gate"], ["in 1", "in other 0"]),
+    (["in 2", "in other 1"], ["up"], ["in 2", "in other 1", "in 3", "grad other 0"]),
+    (["in other 3", "grad 3", "in other 2", "grad 1"], ["down"], ["in other 3", "grad 3"]),
+    (["grad other 3"], ["gu_b"], ["in other 2", "grad 1"]),
+    (["grad 2", "grad other 1"], ["gu_a"], ["grad other 3", "grad 2"]),
+    (["grad other 2"], ["h_b"], ["grad other 2", "grad other 1"]),
+]
 
 
 def ring_body(n, inputs, out_grad, w_gate, w_up, w_down):
     ring = n // 2
-    half = ring // 2
-    last = ring - 1
     across = [(i, i ^ 1) for i in range(n)]
     rows = inputs.shape[0]
 
@@ -239,70 +239,60 @@
     def other_core(x):
         return lax.ppermute(x, "gy", [(0, 1), (1, 0)])
 
-    order = list(range(1, ring)) + [0]
-    early, late = order[:half], order[half:]
+    early, late = (1, 2), (3, 0)
     have = {"in 0": inputs, "grad 0": out_grad, "w_gate": w_gate, "w_up": w_up, "w_down": w_down}
-
-    def blocks_of(name, ks):
-        return [b for k in ks for b in (have[f"{name} {k}"], have[f"{name} other {k}"])]
 
     def source(move):
         name, *other, k = move.split()
-        k = int(k)
-        if other and (name, k) != ("grad", last):
+        if other and move != "grad other 1":
             return f"{name} {k}", swap
-        return " ".join([name, *other, str(k - 1)]), shift
+        by = -1 if k == "3" else 1
+        return " ".join([name, *other, str((int(k) - by) % ring)]), lambda x: shift(x, by)
 
     def products(name, ks, weights, dims, tag):
-        out = gather_matmul(blocks_of(name, ks), [have[w] for w in weights], dims, BF, tag)
+        blocks = [have[f"{name} {side}{k}"] for k in ks for side in ("", "other ")]
+        out = gather_matmul(blocks, [have[w] for w in weights], dims, BF, tag)
         return dict(zip((f"{tag} x", f"{tag} own", f"{tag} send"), out))
-
-    def gate_up(ks, tag):
-        return lambda: products("in", ks, ("gate", "up"), NN, tag)
 
     kernels = {
         "gate": lambda: {"gate": hold(have["w_gate"], 45, "hold_gate")},
         "up": lambda: {"up": hold(have["w_up"], 31, "hold_up")},
         "down": lambda: {"down": hold(have["w_down"], 17, "hold_down")},
-        "a": gate_up(early, "gu_a"),
-        "b": gate_up(late, "gu_b"),
+        "gu_a": lambda: products("in", early, ("gate", "up"), NN, "gu_a"),
+        "gu_b": lambda: products("in", late, ("gate", "up"), NN, "gu_b"),
         "h_a": lambda: products("grad", early, ("down",), NT, "h_a"),
+        "h_b": lambda: products("grad", late, ("down",), NT, "h_b"),
     }
-    for moves, names in gather_stages(ring):
+    moving = {}
+    for starts, names, ends in STAGES:
+        for move in starts:
+            name, how = source(move)
+            moving[move] = how(have[name])
         fresh = {}
-        for move in moves:
-            name, how = source(move)
-            fresh[move] = how(have[name])
         for name in names:
             fresh.update(kernels[name]())
+        for move in ends:
+            fresh[move] = moving.pop(move)
         have.update(fresh)
         have = dict(zip(have, in_order(*have.values())))
 
-    made = {"w_gate": have["gate"], "w_up": have["up"], "x_a": have["gu_a x"], "x_b": have["gu_b x"]}
-    made.update(gu_a=have["gu_a own"], gu_b=have["gu_b own"], gu_send_a=have["gu_a send"], gu_send_b=have["gu_b send"])
-    made.update(grad_a=have["h_a x"], h_a=have["h_a own"], h_send_a=have["h_a send"])
-
-    gu_recv_a, gu_recv_b = other_core(made["gu_send_a"]), other_core(made["gu_send_b"])
-    h_recv_a = other_core(made["h_send_a"])
-    out = products("grad", late, ("down",), NT, "h_b").values()
-    grad_b, h_b, h_send_b, h_a = in_order(*out, made["h_a"])
-    h_recv_b = other_core(h_send_b)
-
-    weights = (made["w_gate"], made["w_up"])
-    out_a = backward(made["gu_a"], gu_recv_a, h_a, h_recv_a, *weights, rows, "back_a")
-    *out_a, h_b = in_order(*out_a, h_b)
+    gu_recv_b, gu_recv_a = other_core(have["gu_b send"]), other_core(have["gu_a send"])
+    h_recv_b = other_core(have["h_b send"])
+    have.update(kernels["h_a"]())
+    have = dict(zip(have, in_order(*have.values())))
+    h_recv_a = other_core(have["h_a send"])
+
+    weights = (have["gate"], have["up"])
     own, sent, recv = {}, {}, {}
-    for i, k in enumerate(order[:half]):
-        own[k], sent[k] = out_a[2 * i : 2 * i + 2]
-    for k in reversed(order[:half]):
-        recv[k] = swap(sent[k])
-    saved_a = out_a[-3:]
-    out_b = backward(made["gu_b"], gu_recv_b, h_b, h_recv_b, *weights, rows, "back_b")
-    recv[half], *out_b = in_order(recv[half], *out_b)
-    for i, k in enumerate(order[half:]):
-        own[k], sent[k] = out_b[2 * i : 2 * i + 2]
-    saved_b = out_b[-3:]
-    hidden, gate_back, up_back = zip(saved_a, saved_b)
+    out_b = backward(have["gu_b own"], gu_recv_b, have["h_b own"], h_recv_b, *weights, rows, "back_b")
+    *out_b, h_own_a = in_order(*out_b, have["h_a own"])
+    own[3], sent[3], own[0], sent[0] = out_b[:4]
+    recv[3] = swap(sent[3])
+    recv[0] = swap(sent[0])
+    out_a = backward(have["gu_a own"], gu_recv_a, h_own_a, h_recv_a, *weights, rows, "back_a")
+    recv[3], *out_a = in_order(recv[3], *out_a)
+    own[1], sent[1], own[2], sent[2] = out_a[:4]
+    hidden, gate_back, up_back = zip(out_a[4:], out_b[4:])
 
     def add(k, *terms):
         total = own[k].astype(F32) + recv[k].astype(F32)
@@ -310,21 +300,18 @@
             total = total + t.astype(F32)
         return total.astype(BF)
 
-    down = shift(add(half), -1)
-    for k in order[half:]:
-        if k:
-            recv[k] = swap(sent[k])
-    (down_wgrad,) = weight_grads(hidden, ((made["grad_a"], grad_b),), 256, "down_wgrad")
-    out = in_order(down, recv[half - 1], recv[half + 1], sent[0], down_wgrad)
-    down, recv[half - 1], recv[half + 1], sent[0], down_wgrad = out
-    for k in range(half - 1, 0, -1):
-        down = shift(add(k, down), -1)
-    ahead = shift(add(half + 1))
-    for k in range(half + 2, ring):
-        ahead = shift(add(k, ahead))
-    recv[0] = swap(sent[0])
-    gate_wgrad, up_wgrad = weight_grads((made["x_a"], made["x_b"]), (gate_back, up_back), 512, "in_wgrads")
-    input_grad = add(0, down, ahead)
+    recv[2] = swap(sent[2])
+    ahead = shift(add(3))
+    recv[1] = swap(sent[1])
+    (down_wgrad,) = weight_grads(hidden, ((have["h_a x"], have["h_b x"]),), 256, "down_wgrad")
+    recv[2], down_wgrad, *gate_back = in_order(recv[2], down_wgrad, *gate_back)
+    back = shift(add(2), -1)
+    x = (have["gu_a x"], have["gu_b x"])
+    (gate_wgrad,) = weight_grads(x, (gate_back,), 512, "gate_wgrad")
+    back, recv[1], gate_wgrad, *up_back = in_order(back, recv[1], gate_wgrad, *up_back)
+    back = shift(add(1, back), -1)
+    (up_wgrad,) = weight_grads(x, (up_back,), 512, "up_wgrad")
+    input_grad = add(0, back, ahead)
     return (input_grad, gate_wgrad, up_wgrad, down_wgrad)
 
 
@@ -355,7 +342,7 @@
 
     def body(inputs, out_grad, w_gate, w_up, w_down):
         args = (inputs, out_grad, w_gate, w_up, w_down)
-        if n % 4 == 0 and n >= 8 and mesh.shape["gy"] == 2 and inputs.shape[0] % 16 == 0:
+        if n == 8 and mesh.shape["gy"] == 2 and inputs.shape[0] % 16 == 0:
             return ring_body(n, *args)
         return plain_body(*args)
 

time: 194 us -> 188 us (0.969)
  waiting for transfers between devices: 45.9 us -> 29.6 us
  starting transfers between devices: 21 us -> 30.7 us
  Pallas kernels: 118 us -> 124 us
  local copies, waits for them, and re-layouts: 6.09 us -> 1.26 us
    ppermute x11, waiting for transfers between devices: 23 us -> 9.17 us  [swap(): return lax.ppermute(x, 'gx', across)]
    ppermute x10, starting transfers between devices: 6.29 us -> 17.3 us  [shift(): return lax.ppermute(x, 'gx', pairs)]
    unnamed x46 -> x38, local copies, waits for them, and re-layouts: 6.09 us -> 1.26 us
    pallas_call x2 -> x3, Pallas kernels: 30.4 us -> 33.9 us  [weight_grads(): call(kernel, name, 2 * tokens * depth * width * count, 2 * depth * width...]
    ppermute x10, waiting for transfers between devices: 22.4 us -> 20.4 us  [shift(): return lax.ppermute(x, 'gx', pairs)]
    pallas_call x4, Pallas kernels: 33.1 us -> 35.2 us  [gather_matmul(): call(kernel, name, 2 * tokens * depth * width * nw, 2 * tokens * depth, 1...]
  transfers between devices with their start and end apart: 25 -> 25, of which waited for: 14 -> 8; matrix products, arithmetic and copies ran while one was open for 0% -> 0% of each run, Pallas kernels for 61% -> 66%
where the time goes in v3:
time: 188 us
  Pallas kernels  124 us (66%)
  starting transfers between devices  30.7 us (16%)
  waiting for transfers between devices  29.6 us (16%)
    pallas_call x2, Pallas kernels, backward(): call(kernel, name, 4 * tokens * depth * width, 20 * tokens * width, 31, g...  39.3 us
    pallas_call x4, Pallas kernels, gather_matmul(): call(kernel, name, 2 * tokens * depth * width * nw, 2 * tokens * depth, 1...  35.2 us
    pallas_call x3, Pallas kernels, weight_grads(): call(kernel, name, 2 * tokens * depth * width * count, 2 * depth * width...  33.9 us
    ppermute x10, waiting for transfers between devices, shift(): return lax.ppermute(x, 'gx', pairs)  20.4 us
    ppermute x10, starting transfers between devices, shift(): return lax.ppermute(x, 'gx', pairs)  17.3 us
    pallas_call x3, Pallas kernels, hold(): call(kernel, name, 1500 * weight.size, 4 * weight.size, vmem, in_specs=[H...  15.5 us
    ppermute x11, starting transfers between devices, swap(): return lax.ppermute(x, 'gx', across)  12.4 us
    ppermute x11, waiting for transfers between devices, swap(): return lax.ppermute(x, 'gx', across)  9.17 us
  transfers between devices with their start and end apart: 25, of which 8 were waited for; matrix products, arithmetic and copies ran while one was open for 0% of the time, Pallas kernels for 66%

profile of v3, /device:TPU:0, one launch (start us, length us, event | category | flops | bytes accessed | tf_op | source)
XLA Modules:
  0.0 187.9 jit_solution(4404792318126121401)
XLA Ops:
  0.6 3.1 %collective-permute-start = (bf16[64,4096]{1,0:T(8,128)(2,1)}, bf16[64,4096]{1,0:T(8,128)(2,1)S(1)}, u32[]{:S(2)}, u32[]{:S(2)}) collective-permute-start(bf16[64,4096]{1,0:T(8,128)(2,1)} %refs_2_), channel_id=1, source_target_pairs={{0,4},{2,6},{4,8},{6,10},{8,12},{10,14},{12,0},{14,2},{1,5},{3,7},... | collective-permute-start | bytes 1572872 | tf_op jit(solution)/shard_map/ppermute | solution.py:234
  3.7 1.5 collective-permute-start.1
  5.2 2.2 %collective-permute-start.4 = (bf16[64,4096]{1,0:T(8,128)(2,1)}, bf16[64,4096]{1,0:T(8,128)(2,1)S(1)}, u32[]{:S(2)}, u32[]{:S(2)}) collective-permute-start(bf16[64,4096]{1,0:T(8,128)(2,1)} %refs_2_), channel_id=1, source_target_pairs={{0,12},{2,14},{4,0},{6,2},{8,4},{10,6},{12,8},{14,10},{1,13},{3,15... | collective-permute-start | bytes 1572872 | tf_op jit(solution)/shard_map/ppermute | solution.py:234
  7.8 5.2 %hold_gate.1.refs_4_ = bf16[4096,1792]{1,0:T(8,128)(2,1)S(1)} custom-call(bf16[4096,1792]{1,0:T(8,128)(2,1)} %w_ref.1), custom_call_target="tpu_custom_call" | custom-call | flops 11010048000 | bytes 29360128 | tf_op jit(solution)/shard_map/hold_gate/pallas_call | solution.py:54
  13.0 5.7 %collective-permute-done.refs_0_ = bf16[64,4096]{1,0:T(8,128)(2,1)S(1)} collective-permute-done((bf16[64,4096]{1,0:T(8,128)(2,1)}, bf16[64,4096]{1,0:T(8,128)(2,1)S(1)}, u32[]{:S(2)}, u32[]{:S(2)}) %collective-permute-start) | collective-permute-done | bytes 524320 | tf_op jit(solution)/shard_map/ppermute | solution.py:234
  18.8 1.6 collective-permute-start.2
  20.3 1.5 collective-permute-start.3
  21.9 5.2 %hold_up.1.refs_5_ = bf16[4096,1792]{1,0:T(8,128)(2,1)S(1)} custom-call(bf16[4096,1792]{1,0:T(8,128)(2,1)} %w_ref.2), custom_call_target="tpu_custom_call" | custom-call | flops 11010048000 | bytes 29360128 | tf_op jit(solution)/shard_map/hold_up/pallas_call | solution.py:54
  27.1 2.8 %collective-permute-done.4.refs_0_ = bf16[64,4096]{1,0:T(8,128)(2,1)S(1)} collective-permute-done((bf16[64,4096]{1,0:T(8,128)(2,1)}, bf16[64,4096]{1,0:T(8,128)(2,1)S(1)}, u32[]{:S(2)}, u32[]{:S(2)}) %collective-permute-start.4) | collective-permute-done | bytes 524320 | tf_op jit(solution)/shard_map/ppermute | solution.py:234
  30.1 10.3 %collective-permute-done.2.refs_2_ = bf16[64,4096]{1,0:T(8,128)(2,1)S(1)} collective-permute-done((bf16[64,4096]{1,0:T(8,128)(2,1)S(1)}, bf16[64,4096]{1,0:T(8,128)(2,1)S(1)}, u32[]{:S(2)}, u32[]{:S(2)}) %collective-permute-start.2) | collective-permute-done | bytes 524320 | tf_op jit(solution)/shard_map/ppermute | solution.py:234
  40.4 1.8 collective-permute-start.7
  42.4 1.5 collective-permute-start.6
  44.4 5.2 %hold_down.1.refs_4_ = bf16[1792,4096]{1,0:T(8,128)(2,1)S(1)} custom-call(bf16[1792,4096]{1,0:T(8,128)(2,1)} %w_ref.3), custom_call_target="tpu_custom_call" | custom-call | flops 11010048000 | bytes 29360128 | tf_op jit(solution)/shard_map/hold_down/pallas_call | solution.py:54
  49.6 7.6 %collective-permute-done.6.refs_1_ = bf16[64,4096]{1,0:T(8,128)(2,1)S(1)} collective-permute-done((bf16[64,4096]{1,0:T(8,128)(2,1)S(1)}, bf16[64,4096]{1,0:T(8,128)(2,1)S(1)}, u32[]{:S(2)}, u32[]{:S(2)}) %collective-permute-start.6) | collective-permute-done | bytes 524320 | tf_op jit(solution)/shard_map/ppermute | solution.py:237
  57.3 1.5 collective-permute-start.10
  58.8 10.1 %gu_b.1 = (bf16[256,4096]{1,0:T(8,128)(2,1)}, f32[2,256,1792]{2,1,0:T(8,128)}, bf16[2,256,1792]{2,1,0:T(8,128)(2,1)}) custom-call(bf16[64,4096]{1,0:T(8,128)(2,1)S(1)} %collective-permute-done.4.refs_0_, bf16[64,4096]{1,0:T(8,128)(2,1)S(1)} %collective-permute-done.6.refs_1_, bf16[64,4096]{1,0:T(8,128)(2,1)S(1)} %copy-done.1, ...), custom_call_target="tpu_custom_call" | custom-call | flops 7516192768 | bytes 2097152 | tf_op jit(solution)/shard_map/gu_b/pallas_call | solution.py:95
  70.0 1.6 collective-permute-start.13
  71.6 10.1 %gu_a.1 = (bf16[256,4096]{1,0:T(8,128)(2,1)}, f32[2,256,1792]{2,1,0:T(8,128)}, bf16[2,256,1792]{2,1,0:T(8,128)(2,1)}) custom-call(bf16[64,4096]{1,0:T(8,128)(2,1)S(1)} %collective-permute-done.refs_0_, bf16[64,4096]{1,0:T(8,128)(2,1)S(1)} %collective-permute-done.3.refs_1_, bf16[64,4096]{1,0:T(8,128)(2,1)S(1)} %collective-permute-done.2.refs_2_, ...), custom_call_target="tpu_custom_call" | custom-call | flops 7516192768 | bytes 2097152 | tf_op jit(solution)/shard_map/gu_a/pallas_call | solution.py:95
  81.7 1.6 collective-permute-done.11.refs_2_
  83.3 1.3 collective-permute-start.12
  84.6 7.6 %h_b.1 = (bf16[256,4096]{1,0:T(8,128)(2,1)}, f32[1,256,1792]{2,1,0:T(8,128)}, bf16[1,256,1792]{2,1,0:T(8,128)(2,1)}) custom-call(bf16[64,4096]{1,0:T(8,128)(2,1)} %collective-permute-done.7.refs_0_, bf16[64,4096]{1,0:T(8,128)(2,1)} %collective-permute-done.10.refs_1_, bf16[64,4096]{1,0:T(8,128)(2,1)S(1)} %copy-done.2, ...), custom_call_target="tpu_custom_call" | custom-call | flops 3758096384 | bytes 2097152 | tf_op jit(solution)/shard_map/h_b/pallas_call | solution.py:95
  93.1 7.3 %h_a.1 = (bf16[256,4096]{1,0:T(8,128)(2,1)}, f32[1,256,1792]{2,1,0:T(8,128)}, bf16[1,256,1792]{2,1,0:T(8,128)(2,1)}) custom-call(bf16[64,4096]{1,0:T(8,128)(2,1)} %collective-permute-done.9.refs_0_, bf16[64,4096]{1,0:T(8,128)(2,1)S(1)} %collective-permute-done.13.refs_1_, bf16[64,4096]{1,0:T(8,128)(2,1)S(1)} %collective-permute-done.11.refs_2_, ...), custom_call_target="tpu_custom_call" | custom-call | flops 3758096384 | bytes 2097152 | tf_op jit(solution)/shard_map/h_a/pallas_call | solution.py:95
  100.8 19.7 %back_b.1 = (bf16[64,4096]{1,0:T(8,128)(2,1)}, bf16[64,4096]{1,0:T(8,128)(2,1)}, bf16[64,4096]{1,0:T(8,128)(2,1)}, bf16[64,4096]{1,0:T(8,128)(2,1)}, bf16[256,17...) custom-call(f32[2,256,1792]{2,1,0:T(8,128)} %get-tuple-element.230.refs_0_, ...), custom_call_target="tpu_custom_call" | custom-call | flops 7516192768 | bytes 9175040 | tf_op jit(solution)/shard_map/back_b/pallas_call | solution.py:157
  120.6 1.4 collective-permute-start.17
  122.7 19.7 %back_a.1 = (bf16[64,4096]{1,0:T(8,128)(2,1)}, bf16[64,4096]{1,0:T(8,128)(2,1)}, bf16[64,4096]{1,0:T(8,128)(2,1)}, bf16[64,4096]{1,0:T(8,128)(2,1)}, bf16[256,17...) custom-call(f32[2,256,1792]{2,1,0:T(8,128)} %get-tuple-element.245.refs_0_, ...), custom_call_target="tpu_custom_call" | custom-call | flops 7516192768 | bytes 9175040 | tf_op jit(solution)/shard_map/back_a/pallas_call | solution.py:157
  145.3 1.2 copy-done.12
  146.5 10.8 %down_wgrad.1 = bf16[1792,4096]{1,0:T(8,128)(2,1)} custom-call(bf16[256,1792]{1,0:T(8,128)(2,1)S(1)} %copy-done.12, bf16[256,1792]{1,0:T(8,128)(2,1)S(1)} %copy-done.10, bf16[256,4096]{1,0:T(8,128)(2,1)S(1)} %copy-done.6, bf16[256,4096]{1,0:T(8,128)(2,1)S(1)} %copy-done.5), custom_call_target="tpu_custom_call" | custom-call | flops 7516192768 | bytes 14680064 | tf_op jit(solution)/shard_map/down_wgrad/pallas_call | solution.py:199
  158.5 3.2 %collective-permute-start.21 = (bf16[64,4096]{1,0:T(8,128)(2,1)S(1)}, bf16[64,4096]{1,0:T(8,128)(2,1)S(1)}, u32[]{:S(2)}, u32[]{:S(2)}) collective-permute-start(bf16[64,4096]{1,0:T(8,128)(2,1)S(1)} %add_convert_fusion.3), channel_id=1, source_target_pairs={{0,12},{2,14},{4,0},{6,2},{8,4},{10,6},{12,8},{14,10},{1,13},{3,15... | collective-permute-start | bytes 1572872 | tf_op jit(solution)/shard_map/ppermute | solution.py:234
  161.7 11.5 %gate_wgrad.1 = bf16[4096,1792]{1,0:T(8,128)(2,1)} custom-call(bf16[256,4096]{1,0:T(8,128)(2,1)S(1)} %copy-done.4, bf16[256,4096]{1,0:T(8,128)(2,1)S(1)} %copy-done.3, bf16[256,1792]{1,0:T(8,128)(2,1)S(1)} %copy-done.11, bf16[256,1792]{1,0:T(8,128)(2,1)S(1)} %copy-done.8), custom_call_target="tpu_custom_call" | custom-call | flops 7516192768 | bytes 14680064 | tf_op jit(solution)/shard_map/gate_wgrad/pallas_call | solution.py:199
  173.5 1.8 collective-permute-start.23
  175.3 11.5 %up_wgrad.1 = bf16[4096,1792]{1,0:T(8,128)(2,1)} custom-call(bf16[256,4096]{1,0:T(8,128)(2,1)S(1)} %copy-done.4, bf16[256,4096]{1,0:T(8,128)(2,1)S(1)} %copy-done.3, bf16[256,1792]{1,0:T(8,128)(2,1)S(1)} %copy-done.9, bf16[256,1792]{1,0:T(8,128)(2,1)S(1)} %copy-done.7), custom_call_target="tpu_custom_call" | custom-call | flops 7516192768 | bytes 14680064 | tf_op jit(solution)/shard_map/up_wgrad/pallas_call | solution.py:199
  186.8 1.1 add_convert_fusion
  (72 shorter events, 8.8 us)
Async XLA Ops:
  0.6 18.1 %collective-permute-start = (bf16[64,4096]{1,0:T(8,128)(2,1)}, bf16[64,4096]{1,0:T(8,128)(2,1)S(1)}, u32[]{:S(2)}, u32[]{:S(2)}) collective-permute-start(bf16[64,4096]{1,0:T(8,128)(2,1)} %refs_2_), channel_id=1, source_target_pairs={{0,4},{2,6},{4,8},{6,10},{8,12},{10,14},{12,0},{14,2},{1,5},{3,7},... | collective-permute-start | bytes 1572872 | tf_op jit(solution)/shard_map/ppermute | solution.py:234
  3.7 15.1 %collective-permute-start.1 = (bf16[64,4096]{1,0:T(8,128)(2,1)}, bf16[64,4096]{1,0:T(8,128)(2,1)S(1)}, u32[]{:S(2)}, u32[]{:S(2)}) collective-permute-start(bf16[64,4096]{1,0:T(8,128)(2,1)} %refs_2_), channel_id=1, source_target_pairs={{0,2},{2,0},{4,6},{6,4},{8,10},{10,8},{12,14},{14,12},{1,3},{3,1},... | collective-permute-start | bytes 1572872 | tf_op jit(solution)/shard_map/ppermute | solution.py:237
  5.2 24.7 %collective-permute-start.4 = (bf16[64,4096]{1,0:T(8,128)(2,1)}, bf16[64,4096]{1,0:T(8,128)(2,1)S(1)}, u32[]{:S(2)}, u32[]{:S(2)}) collective-permute-start(bf16[64,4096]{1,0:T(8,128)(2,1)} %refs_2_), channel_id=1, source_target_pairs={{0,12},{2,14},{4,0},{6,2},{8,4},{10,6},{12,8},{14,10},{1,13},{3,15... | collective-permute-start | bytes 1572872 | tf_op jit(solution)/shard_map/ppermute | solution.py:234
  7.5 22.6 %collective-permute-start.5 = (bf16[64,4096]{1,0:T(8,128)(2,1)}, bf16[64,4096]{1,0:T(8,128)(2,1)}, u32[]{:S(2)}, u32[]{:S(2)}) collective-permute-start(bf16[64,4096]{1,0:T(8,128)(2,1)} %refs_2_.1), channel_id=1, source_target_pairs={{0,2},{2,0},{4,6},{6,4},{8,10},{10,8},{12,14},{14,12},{1,3},{3,1},... | collective-permute-start | bytes 1572872 | tf_op jit(solution)/shard_map/ppermute | solution.py:237
  13.0 27.4 %copy-start.2 = (bf16[64,4096]{1,0:T(8,128)(2,1)S(1)}, bf16[64,4096]{1,0:T(8,128)(2,1)}, u32[]{:S(2)}) copy-start(bf16[64,4096]{1,0:T(8,128)(2,1)} %refs_2_.1) | copy-start | bytes 1572868
  18.8 21.6 %collective-permute-start.2 = (bf16[64,4096]{1,0:T(8,128)(2,1)S(1)}, bf16[64,4096]{1,0:T(8,128)(2,1)S(1)}, u32[]{:S(2)}, u32[]{:S(2)}) collective-permute-start(bf16[64,4096]{1,0:T(8,128)(2,1)S(1)} %collective-permute-done.refs_0_), channel_id=1, source_target_pairs={{0,4},{2,6},{4,8},{6,10},{8,12},{10,14},{12,0},{14,2},{1,5},{3,7},... | collective-permute-start | bytes 1572872 | tf_op jit(solution)/shard_map/ppermute | solution.py:234
  20.3 20.0 %collective-permute-start.3 = (bf16[64,4096]{1,0:T(8,128)(2,1)S(1)}, bf16[64,4096]{1,0:T(8,128)(2,1)S(1)}, u32[]{:S(2)}, u32[]{:S(2)}) collective-permute-start(bf16[64,4096]{1,0:T(8,128)(2,1)S(1)} %collective-permute-done.refs_0_), channel_id=1, source_target_pairs={{0,2},{2,0},{4,6},{6,4},{8,10},{10,8},{12,14},{14,12},{1,3},{3,1},... | collective-permute-start | bytes 1572872 | tf_op jit(solution)/shard_map/ppermute | solution.py:237
  27.1 44.5 %copy-start = (bf16[4096,1792]{1,0:T(8,128)(2,1)}, bf16[4096,1792]{1,0:T(8,128)(2,1)S(1)}, u32[]{:S(2)}) copy-start(bf16[4096,1792]{1,0:T(8,128)(2,1)S(1)} %hold_up.1.refs_5_) | copy-start | bytes 44040196
  27.1 31.7 %copy-start.1 = (bf16[64,4096]{1,0:T(8,128)(2,1)S(1)}, bf16[64,4096]{1,0:T(8,128)(2,1)}, u32[]{:S(2)}) copy-start(bf16[64,4096]{1,0:T(8,128)(2,1)} %refs_2_) | copy-start | bytes 1572868
  40.4 16.9 %collective-permute-start.7 = (bf16[64,4096]{1,0:T(8,128)(2,1)S(1)}, bf16[64,4096]{1,0:T(8,128)(2,1)}, u32[]{:S(2)}, u32[]{:S(2)}) collective-permute-start(bf16[64,4096]{1,0:T(8,128)(2,1)S(1)} %copy-done.2), channel_id=1, source_target_pairs={{0,12},{2,14},{4,0},{6,2},{8,4},{10,6},{12,8},{14,10},{1,13},{3,15... | collective-permute-start | bytes 1572872 | tf_op jit(solution)/shard_map/ppermute | solution.py:234
  42.2 26.8 %collective-permute-start.9 = (bf16[64,4096]{1,0:T(8,128)(2,1)S(1)}, bf16[64,4096]{1,0:T(8,128)(2,1)}, u32[]{:S(2)}, u32[]{:S(2)}) collective-permute-start(bf16[64,4096]{1,0:T(8,128)(2,1)S(1)} %copy-done.2), channel_id=1, source_target_pairs={{0,4},{2,6},{4,8},{6,10},{8,12},{10,14},{12,0},{14,2},{1,5},{3,7},... | collective-permute-start | bytes 1572872 | tf_op jit(solution)/shard_map/ppermute | solution.py:234
  42.4 14.9 %collective-permute-start.6 = (bf16[64,4096]{1,0:T(8,128)(2,1)S(1)}, bf16[64,4096]{1,0:T(8,128)(2,1)S(1)}, u32[]{:S(2)}, u32[]{:S(2)}) collective-permute-start(bf16[64,4096]{1,0:T(8,128)(2,1)S(1)} %collective-permute-done.4.refs_0_), channel_id=1, source_target_pairs={{0,2},{2,0},{4,6},{6,4},{8,10},{10,8},{12,14},{14,12},{1,3},{3,1},... | collective-permute-start | bytes 1572872 | tf_op jit(solution)/shard_map/ppermute | solution.py:237
  43.9 25.0 %collective-permute-start.8 = (bf16[64,4096]{1,0:T(8,128)(2,1)S(1)}, bf16[64,4096]{1,0:T(8,128)(2,1)S(1)}, u32[]{:S(2)}, u32[]{:S(2)}) collective-permute-start(bf16[64,4096]{1,0:T(8,128)(2,1)S(1)} %collective-permute-done.2.refs_2_), channel_id=1, source_target_pairs={{0,2},{2,0},{4,6},{6,4},{8,10},{10,8},{12,14},{14,12},{1,3},{3,1},... | collective-permute-start | bytes 1572872 | tf_op jit(solution)/shard_map/ppermute | solution.py:237
  57.3 24.4 %collective-permute-start.10 = (bf16[64,4096]{1,0:T(8,128)(2,1)}, bf16[64,4096]{1,0:T(8,128)(2,1)}, u32[]{:S(2)}, u32[]{:S(2)}) collective-permute-start(bf16[64,4096]{1,0:T(8,128)(2,1)} %collective-permute-done.7.refs_0_), channel_id=1, source_target_pairs={{0,2},{2,0},{4,6},{6,4},{8,10},{10,8},{12,14},{14,12},{1,3},{3,1},... | collective-permute-start | bytes 1572872 | tf_op jit(solution)/shard_map/ppermute | solution.py:237
  69.0 14.3 %collective-permute-start.11 = (bf16[64,4096]{1,0:T(8,128)(2,1)}, bf16[64,4096]{1,0:T(8,128)(2,1)S(1)}, u32[]{:S(2)}, u32[]{:S(2)}) collective-permute-start(bf16[64,4096]{1,0:T(8,128)(2,1)} %collective-permute-done.9.refs_0_), channel_id=1, source_target_pairs={{0,4},{2,6},{4,8},{6,10},{8,12},{10,14},{12,0},{14,2},{1,5},{3,7},... | collective-permute-start | bytes 1572872 | tf_op jit(solution)/shard_map/ppermute | solution.py:234
  70.0 22.2 %collective-permute-start.13 = (bf16[64,4096]{1,0:T(8,128)(2,1)}, bf16[64,4096]{1,0:T(8,128)(2,1)S(1)}, u32[]{:S(2)}, u32[]{:S(2)}) collective-permute-start(bf16[64,4096]{1,0:T(8,128)(2,1)} %collective-permute-done.5.refs_3_), channel_id=1, source_target_pairs={{0,4},{2,6},{4,8},{6,10},{8,12},{10,14},{12,0},{14,2},{1,5},{3,7},... | collective-permute-start | bytes 1572872 | tf_op jit(solution)/shard_map/ppermute | solution.py:234
  83.3 9.2 %collective-permute-start.12 = (bf16[64,4096]{1,0:T(8,128)(2,1)S(1)}, bf16[64,4096]{1,0:T(8,128)(2,1)S(1)}, u32[]{:S(2)}, u32[]{:S(2)}) collective-permute-start(bf16[64,4096]{1,0:T(8,128)(2,1)S(1)} %collective-permute-done.11.refs_2_), channel_id=1, source_target_pairs={{0,2},{2,0},{4,6},{6,4},{8,10},{10,8},{12,14},{14,12},{1,3},{3,1},... | collective-permute-start | bytes 1572872 | tf_op jit(solution)/shard_map/ppermute | solution.py:237
  92.5 8.4 %collective-permute-start.14 = (bf16[2,256,1792]{2,1,0:T(8,128)(2,1)S(1)}, bf16[2,256,1792]{2,1,0:T(8,128)(2,1)S(1)}, u32[]{:S(2)}, u32[]{:S(2)}) collective-permute-start(bf16[2,256,1792]{2,1,0:T(8,128)(2,1)S(1)} %copy-done.18), channel_id=1, source_target_pairs={{0,1},{1,0},{2,3},{3,2},{4,5},{5,4},{6,7},{7,6},{8,9},{9,8},{10,11... | collective-permute-start | bytes 5505032 | tf_op jit(solution)/shard_map/ppermute | solution.py:240
  92.5 30.2 %collective-permute-start.18 = (bf16[2,256,1792]{2,1,0:T(8,128)(2,1)S(1)}, bf16[2,256,1792]{2,1,0:T(8,128)(2,1)S(1)}, u32[]{:S(2)}, u32[]{:S(2)}) collective-permute-start(bf16[2,256,1792]{2,1,0:T(8,128)(2,1)S(1)} %copy-done.17), channel_id=1, source_target_pairs={{0,1},{1,0},{2,3},{3,2},{4,5},{5,4},{6,7},{7,6},{8,9},{9,8},{10,11... | collective-permute-start | bytes 5505032 | tf_op jit(solution)/shard_map/ppermute | solution.py:240
  93.0 7.9 %collective-permute-start.15 = (bf16[1,256,1792]{2,1,0:T(8,128)(2,1)}, bf16[1,256,1792]{2,1,0:T(8,128)(2,1)S(1)}, u32[]{:S(2)}, u32[]{:S(2)}) collective-permute-start(bf16[1,256,1792]{2,1,0:T(8,128)(2,1)} %get-tuple-element.224), channel_id=1, source_target_pairs={{0,1},{1,0},{2,3},{3,2},{4,5},{5,4},{6,7},{7,6},{8,9},{9,8},{10,11... | collective-permute-start | bytes 2752520 | tf_op jit(solution)/shard_map/ppermute | solution.py:240
  100.3 22.3 %collective-permute-start.19 = (bf16[1,256,1792]{2,1,0:T(8,128)(2,1)}, bf16[1,256,1792]{2,1,0:T(8,128)(2,1)S(1)}, u32[]{:S(2)}, u32[]{:S(2)}) collective-permute-start(bf16[1,256,1792]{2,1,0:T(8,128)(2,1)} %get-tuple-element.247), channel_id=1, source_target_pairs={{0,1},{1,0},{2,3},{3,2},{4,5},{5,4},{6,7},{7,6},{8,9},{9,8},{10,11... | collective-permute-start | bytes 2752520 | tf_op jit(solution)/shard_map/ppermute | solution.py:240
  120.5 21.8 %copy-start.14 = (bf16[64,4096]{1,0:T(8,128)(2,1)S(1)}, bf16[64,4096]{1,0:T(8,128)(2,1)}, u32[]{:S(2)}) copy-start(bf16[64,4096]{1,0:T(8,128)(2,1)} %get-tuple-element.274) | copy-start | bytes 1572868
  120.5 24.7 %copy-start.5 = (bf16[256,4096]{1,0:T(8,128)(2,1)S(1)}, bf16[256,4096]{1,0:T(8,128)(2,1)}, u32[]{:S(2)}) copy-start(bf16[256,4096]{1,0:T(8,128)(2,1)} %get-tuple-element.261.refs_3_) | copy-start | bytes 6291460
  120.5 24.7 %copy-start.6 = (bf16[256,4096]{1,0:T(8,128)(2,1)S(1)}, bf16[256,4096]{1,0:T(8,128)(2,1)}, u32[]{:S(2)}) copy-start(bf16[256,4096]{1,0:T(8,128)(2,1)} %get-tuple-element.260.refs_2_) | copy-start | bytes 6291460
  120.6 24.7 %copy-start.10 = (bf16[256,1792]{1,0:T(8,128)(2,1)S(1)}, bf16[256,1792]{1,0:T(8,128)(2,1)}, u32[]{:S(2)}) copy-start(bf16[256,1792]{1,0:T(8,128)(2,1)} %get-tuple-element.259.refs_1_) | copy-start | bytes 2752516
  120.6 21.8 %collective-permute-start.17 = (bf16[64,4096]{1,0:T(8,128)(2,1)}, bf16[64,4096]{1,0:T(8,128)(2,1)S(1)}, u32[]{:S(2)}, u32[]{:S(2)}) collective-permute-start(bf16[64,4096]{1,0:T(8,128)(2,1)} %get-tuple-element.244), channel_id=1, source_target_pairs={{0,2},{2,0},{4,6},{6,4},{8,10},{10,8},{12,14},{14,12},{1,3},{3,1},... | collective-permute-start | bytes 1572872 | tf_op jit(solution)/shard_map/ppermute | solution.py:237
  121.9 64.9 %collective-permute-start.16 = (bf16[64,4096]{1,0:T(8,128)(2,1)}, bf16[64,4096]{1,0:T(8,128)(2,1)S(1)}, u32[]{:S(2)}, u32[]{:S(2)}) collective-permute-start(bf16[64,4096]{1,0:T(8,128)(2,1)} %get-tuple-element.243), channel_id=1, source_target_pairs={{0,2},{2,0},{4,6},{6,4},{8,10},{10,8},{12,14},{14,12},{1,3},{3,1},... | collective-permute-start | bytes 1572872 | tf_op jit(solution)/shard_map/ppermute | solution.py:237
  142.5 44.3 %collective-permute-start.24 = (bf16[64,4096]{1,0:T(8,128)(2,1)S(1)}, bf16[64,4096]{1,0:T(8,128)(2,1)S(1)}, u32[]{:S(2)}, u32[]{:S(2)}) collective-permute-start(bf16[64,4096]{1,0:T(8,128)(2,1)S(1)} %add_convert_fusion.1), channel_id=1, source_target_pairs={{0,4},{2,6},{4,8},{6,10},{8,12},{10,14},{12,0},{14,2},{1,5},{3,7},... | collective-permute-start | bytes 1572872 | tf_op jit(solution)/shard_map/ppermute | solution.py:234
  143.2 15.1 %collective-permute-start.20 = (bf16[64,4096]{1,0:T(8,128)(2,1)}, bf16[64,4096]{1,0:T(8,128)(2,1)S(1)}, u32[]{:S(2)}, u32[]{:S(2)}) collective-permute-start(bf16[64,4096]{1,0:T(8,128)(2,1)} %get-tuple-element.257), channel_id=1, source_target_pairs={{0,2},{2,0},{4,6},{6,4},{8,10},{10,8},{12,14},{14,12},{1,3},{3,1},... | collective-permute-start | bytes 1572872 | tf_op jit(solution)/shard_map/ppermute | solution.py:237
  144.3 29.0 %collective-permute-start.22 = (bf16[64,4096]{1,0:T(8,128)(2,1)}, bf16[64,4096]{1,0:T(8,128)(2,1)S(1)}, u32[]{:S(2)}, u32[]{:S(2)}) collective-permute-start(bf16[64,4096]{1,0:T(8,128)(2,1)} %get-tuple-element.265), channel_id=1, source_target_pairs={{0,2},{2,0},{4,6},{6,4},{8,10},{10,8},{12,14},{14,12},{1,3},{3,1},... | collective-permute-start | bytes 1572872 | tf_op jit(solution)/shard_map/ppermute | solution.py:237
  158.5 14.8 %collective-permute-start.21 = (bf16[64,4096]{1,0:T(8,128)(2,1)S(1)}, bf16[64,4096]{1,0:T(8,128)(2,1)S(1)}, u32[]{:S(2)}, u32[]{:S(2)}) collective-permute-start(bf16[64,4096]{1,0:T(8,128)(2,1)S(1)} %add_convert_fusion.3), channel_id=1, source_target_pairs={{0,12},{2,14},{4,0},{6,2},{8,4},{10,6},{12,8},{14,10},{1,13},{3,15... | collective-permute-start | bytes 1572872 | tf_op jit(solution)/shard_map/ppermute | solution.py:234
  173.5 13.4 %collective-permute-start.23 = (bf16[64,4096]{1,0:T(8,128)(2,1)S(1)}, bf16[64,4096]{1,0:T(8,128)(2,1)S(1)}, u32[]{:S(2)}, u32[]{:S(2)}) collective-permute-start(bf16[64,4096]{1,0:T(8,128)(2,1)S(1)} %add_convert_fusion.2), channel_id=1, source_target_pairs={{0,12},{2,14},{4,0},{6,2},{8,4},{10,6},{12,8},{14,10},{1,13},{3,15... | collective-permute-start | bytes 1572872 | tf_op jit(solution)/shard_map/ppermute | solution.py:234
  (12 other events, 174.2 us)

commit v4 on v3

--- a/solution.py
+++ b/solution.py
@@ -119,7 +119,7 @@
     def kernel(*refs):
         own_gu_ref, recv_gu_ref, own_h_ref, recv_h_ref, wg_ref, wu_ref = refs[:6]
         block_refs = refs[6 : 6 + blocks]
-        hidden_ref, gb_ref, ub_ref, gb_t, ub_t = refs[6 + blocks :]
+        hidden_ref, gb_ref, ub_ref, gb_all, ub_all = refs[6 + blocks :]
         step = pl.program_id(0)
 
         @pl.when(step < act_steps)
@@ -139,14 +139,14 @@
                 up_back = (hidden_grad * silu_val).astype(BF)
                 gb_ref[:, at] = gate_back
                 ub_ref[:, at] = up_back
-                lines = pl.ds(pl.multiple_of(step * act_tile + i * part, part), part)
-                gb_t[lines, :] = gate_back.T
-                ub_t[lines, :] = up_back.T
+                cols = pl.ds(pl.multiple_of(step * act_tile + i * part, part), part)
+                gb_all[:, cols] = gate_back
+                ub_all[:, cols] = up_back
 
         @pl.when(step >= act_steps)
         def _():
             at = pl.ds(pl.multiple_of((step - act_steps) * tile, tile), tile)
-            out = (dot(wg_ref[at, :], gb_t[...], NN) + dot(wu_ref[at, :], ub_t[...], NN)).T
+            out = dot(gb_all[...], wg_ref[at, :], NT) + dot(ub_all[...], wu_ref[at, :], NT)
             for i, ref in enumerate(block_refs):
                 ref[...] = out[i * rows : (i + 1) * rows].astype(BF)
 
@@ -164,7 +164,7 @@
         in_specs=[act_spec(2), act_spec(2), act_spec(1), act_spec(1), VMEM_SPEC, VMEM_SPEC],
         out_specs=[pl.BlockSpec((rows, tile), lambda j: (0, jnp.maximum(j - act_steps, 0)))] * blocks + [act_out] * 3,
         out_shape=[pltpu.HBM((rows, depth), BF)] * blocks + [pltpu.HBM((tokens, width), BF)] * 3,
-        scratch_shapes=[pltpu.VMEM((width, tokens), BF)] * 2,
+        scratch_shapes=[pltpu.VMEM((tokens, width), BF)] * 2,
     )(in_hbm(own_gu), recv_gu, in_hbm(own_h), recv_h, w_gate, w_up)
 
 

time: 188 us -> 187 us (level)
  Pallas kernels: 124 us -> 122 us
where the time goes in v4:
time: 187 us; the launch traced here: 186 us
  Pallas kernels  122 us (65%)
  starting transfers between devices  30.2 us (16%)
  waiting for transfers between devices  30.1 us (16%)
    pallas_call x2, Pallas kernels, backward(): call(kernel, name, 4 * tokens * depth * width, 20 * tokens * width, 31, g...  37.9 us
    pallas_call x4, Pallas kernels, gather_matmul(): call(kernel, name, 2 * tokens * depth * width * nw, 2 * tokens * depth, 1...  35.2 us
    pallas_call x3, Pallas kernels, weight_grads(): call(kernel, name, 2 * tokens * depth * width * count, 2 * depth * width...  33.9 us
    ppermute x10, waiting for transfers between devices, shift(): return lax.ppermute(x, 'gx', pairs)  20.4 us
    ppermute x10, starting transfers between devices, shift(): return lax.ppermute(x, 'gx', pairs)  16.7 us
    pallas_call x3, Pallas kernels, hold(): call(kernel, name, 1500 * weight.size, 4 * weight.size, vmem, in_specs=[H...  15.5 us
    ppermute x11, starting transfers between devices, swap(): return lax.ppermute(x, 'gx', across)  12.4 us
    ppermute x11, waiting for transfers between devices, swap(): return lax.ppermute(x, 'gx', across)  9.7 us
  transfers between devices with their start and end apart: 25, of which 8 were waited for; matrix products, arithmetic and copies ran while one was open for 0% of the time, Pallas kernels for 66%

profile of v4, /device:TPU:0, one launch (start us, length us, event | category | flops | bytes accessed | tf_op | source)
XLA Modules:
  0.0 186.4 jit_solution(14643793074323338272)
XLA Ops:
  0.6 3.1 %collective-permute-start = (bf16[64,4096]{1,0:T(8,128)(2,1)}, bf16[64,4096]{1,0:T(8,128)(2,1)S(1)}, u32[]{:S(2)}, u32[]{:S(2)}) collective-permute-start(bf16[64,4096]{1,0:T(8,128)(2,1)} %refs_2_), channel_id=1, source_target_pairs={{0,4},{2,6},{4,8},{6,10},{8,12},{10,14},{12,0},{14,2},{1,5},{3,7},... | collective-permute-start | bytes 1572872 | tf_op jit(solution)/shard_map/ppermute | solution.py:234
  3.7 1.5 collective-permute-start.1
  5.2 2.2 %collective-permute-start.4 = (bf16[64,4096]{1,0:T(8,128)(2,1)}, bf16[64,4096]{1,0:T(8,128)(2,1)S(1)}, u32[]{:S(2)}, u32[]{:S(2)}) collective-permute-start(bf16[64,4096]{1,0:T(8,128)(2,1)} %refs_2_), channel_id=1, source_target_pairs={{0,12},{2,14},{4,0},{6,2},{8,4},{10,6},{12,8},{14,10},{1,13},{3,15... | collective-permute-start | bytes 1572872 | tf_op jit(solution)/shard_map/ppermute | solution.py:234
  7.8 5.2 %hold_gate.1.refs_4_ = bf16[4096,1792]{1,0:T(8,128)(2,1)S(1)} custom-call(bf16[4096,1792]{1,0:T(8,128)(2,1)} %w_ref.1), custom_call_target="tpu_custom_call" | custom-call | flops 11010048000 | bytes 29360128 | tf_op jit(solution)/shard_map/hold_gate/pallas_call | solution.py:54
  13.0 5.7 %collective-permute-done.refs_0_ = bf16[64,4096]{1,0:T(8,128)(2,1)S(1)} collective-permute-done((bf16[64,4096]{1,0:T(8,128)(2,1)}, bf16[64,4096]{1,0:T(8,128)(2,1)S(1)}, u32[]{:S(2)}, u32[]{:S(2)}) %collective-permute-start) | collective-permute-done | bytes 524320 | tf_op jit(solution)/shard_map/ppermute | solution.py:234
  18.8 1.6 collective-permute-start.2
  20.3 1.5 collective-permute-start.3
  21.9 5.2 %hold_up.1.refs_5_ = bf16[4096,1792]{1,0:T(8,128)(2,1)S(1)} custom-call(bf16[4096,1792]{1,0:T(8,128)(2,1)} %w_ref.2), custom_call_target="tpu_custom_call" | custom-call | flops 11010048000 | bytes 29360128 | tf_op jit(solution)/shard_map/hold_up/pallas_call | solution.py:54
  27.1 2.8 %collective-permute-done.4.refs_0_ = bf16[64,4096]{1,0:T(8,128)(2,1)S(1)} collective-permute-done((bf16[64,4096]{1,0:T(8,128)(2,1)}, bf16[64,4096]{1,0:T(8,128)(2,1)S(1)}, u32[]{:S(2)}, u32[]{:S(2)}) %collective-permute-start.4) | collective-permute-done | bytes 524320 | tf_op jit(solution)/shard_map/ppermute | solution.py:234
  30.1 10.3 %collective-permute-done.2.refs_2_ = bf16[64,4096]{1,0:T(8,128)(2,1)S(1)} collective-permute-done((bf16[64,4096]{1,0:T(8,128)(2,1)S(1)}, bf16[64,4096]{1,0:T(8,128)(2,1)S(1)}, u32[]{:S(2)}, u32[]{:S(2)}) %collective-permute-start.2) | collective-permute-done | bytes 524320 | tf_op jit(solution)/shard_map/ppermute | solution.py:234
  40.4 1.8 collective-permute-start.7
  42.4 1.5 collective-permute-start.6
  44.4 5.2 %hold_down.1.refs_4_ = bf16[1792,4096]{1,0:T(8,128)(2,1)S(1)} custom-call(bf16[1792,4096]{1,0:T(8,128)(2,1)} %w_ref.3), custom_call_target="tpu_custom_call" | custom-call | flops 11010048000 | bytes 29360128 | tf_op jit(solution)/shard_map/hold_down/pallas_call | solution.py:54
  49.6 7.6 %collective-permute-done.6.refs_1_ = bf16[64,4096]{1,0:T(8,128)(2,1)S(1)} collective-permute-done((bf16[64,4096]{1,0:T(8,128)(2,1)S(1)}, bf16[64,4096]{1,0:T(8,128)(2,1)S(1)}, u32[]{:S(2)}, u32[]{:S(2)}) %collective-permute-start.6) | collective-permute-done | bytes 524320 | tf_op jit(solution)/shard_map/ppermute | solution.py:237
  57.3 1.5 collective-permute-start.10
  58.8 10.1 %gu_b.1 = (bf16[256,4096]{1,0:T(8,128)(2,1)}, f32[2,256,1792]{2,1,0:T(8,128)}, bf16[2,256,1792]{2,1,0:T(8,128)(2,1)}) custom-call(bf16[64,4096]{1,0:T(8,128)(2,1)S(1)} %collective-permute-done.4.refs_0_, bf16[64,4096]{1,0:T(8,128)(2,1)S(1)} %collective-permute-done.6.refs_1_, bf16[64,4096]{1,0:T(8,128)(2,1)S(1)} %copy-done.1, ...), custom_call_target="tpu_custom_call" | custom-call | flops 7516192768 | bytes 2097152 | tf_op jit(solution)/shard_map/gu_b/pallas_call | solution.py:95
  70.0 1.6 collective-permute-start.13
  71.6 10.1 %gu_a.1 = (bf16[256,4096]{1,0:T(8,128)(2,1)}, f32[2,256,1792]{2,1,0:T(8,128)}, bf16[2,256,1792]{2,1,0:T(8,128)(2,1)}) custom-call(bf16[64,4096]{1,0:T(8,128)(2,1)S(1)} %collective-permute-done.refs_0_, bf16[64,4096]{1,0:T(8,128)(2,1)S(1)} %collective-permute-done.3.refs_1_, bf16[64,4096]{1,0:T(8,128)(2,1)S(1)} %collective-permute-done.2.refs_2_, ...), custom_call_target="tpu_custom_call" | custom-call | flops 7516192768 | bytes 2097152 | tf_op jit(solution)/shard_map/gu_a/pallas_call | solution.py:95
  81.7 1.6 collective-permute-done.11.refs_2_
  83.3 1.3 collective-permute-start.12
  84.6 7.6 %h_b.1 = (bf16[256,4096]{1,0:T(8,128)(2,1)}, f32[1,256,1792]{2,1,0:T(8,128)}, bf16[1,256,1792]{2,1,0:T(8,128)(2,1)}) custom-call(bf16[64,4096]{1,0:T(8,128)(2,1)} %collective-permute-done.7.refs_0_, bf16[64,4096]{1,0:T(8,128)(2,1)} %collective-permute-done.10.refs_1_, bf16[64,4096]{1,0:T(8,128)(2,1)S(1)} %copy-done.2, ...), custom_call_target="tpu_custom_call" | custom-call | flops 3758096384 | bytes 2097152 | tf_op jit(solution)/shard_map/h_b/pallas_call | solution.py:95
  93.1 7.3 %h_a.1 = (bf16[256,4096]{1,0:T(8,128)(2,1)}, f32[1,256,1792]{2,1,0:T(8,128)}, bf16[1,256,1792]{2,1,0:T(8,128)(2,1)}) custom-call(bf16[64,4096]{1,0:T(8,128)(2,1)} %collective-permute-done.9.refs_0_, bf16[64,4096]{1,0:T(8,128)(2,1)S(1)} %collective-permute-done.13.refs_1_, bf16[64,4096]{1,0:T(8,128)(2,1)S(1)} %collective-permute-done.11.refs_2_, ...), custom_call_target="tpu_custom_call" | custom-call | flops 3758096384 | bytes 2097152 | tf_op jit(solution)/shard_map/h_a/pallas_call | solution.py:95
  100.8 19.0 %back_b.1 = (bf16[64,4096]{1,0:T(8,128)(2,1)}, bf16[64,4096]{1,0:T(8,128)(2,1)}, bf16[64,4096]{1,0:T(8,128)(2,1)}, bf16[64,4096]{1,0:T(8,128)(2,1)}, bf16[256,17...) custom-call(f32[2,256,1792]{2,1,0:T(8,128)} %get-tuple-element.230.refs_0_, ...), custom_call_target="tpu_custom_call" | custom-call | flops 7516192768 | bytes 9175040 | tf_op jit(solution)/shard_map/back_b/pallas_call | solution.py:157
  119.9 1.4 collective-permute-start.17
  122.0 18.9 %back_a.1 = (bf16[64,4096]{1,0:T(8,128)(2,1)}, bf16[64,4096]{1,0:T(8,128)(2,1)}, bf16[64,4096]{1,0:T(8,128)(2,1)}, bf16[64,4096]{1,0:T(8,128)(2,1)}, bf16[256,17...) custom-call(f32[2,256,1792]{2,1,0:T(8,128)} %get-tuple-element.245.refs_0_, ...), custom_call_target="tpu_custom_call" | custom-call | flops 7516192768 | bytes 9175040 | tf_op jit(solution)/shard_map/back_a/pallas_call | solution.py:157
  143.8 1.2 copy-done.12
  145.0 10.8 %down_wgrad.1 = bf16[1792,4096]{1,0:T(8,128)(2,1)} custom-call(bf16[256,1792]{1,0:T(8,128)(2,1)S(1)} %copy-done.12, bf16[256,1792]{1,0:T(8,128)(2,1)S(1)} %copy-done.10, bf16[256,4096]{1,0:T(8,128)(2,1)S(1)} %copy-done.6, bf16[256,4096]{1,0:T(8,128)(2,1)S(1)} %copy-done.5), custom_call_target="tpu_custom_call" | custom-call | flops 7516192768 | bytes 14680064 | tf_op jit(solution)/shard_map/down_wgrad/pallas_call | solution.py:199
  155.8 1.6 collective-permute-done.20
  157.5 2.7 %collective-permute-start.21 = (bf16[64,4096]{1,0:T(8,128)(2,1)S(1)}, bf16[64,4096]{1,0:T(8,128)(2,1)S(1)}, u32[]{:S(2)}, u32[]{:S(2)}) collective-permute-start(bf16[64,4096]{1,0:T(8,128)(2,1)S(1)} %add_convert_fusion.3), channel_id=1, source_target_pairs={{0,12},{2,14},{4,0},{6,2},{8,4},{10,6},{12,8},{14,10},{1,13},{3,15... | collective-permute-start | bytes 1572872 | tf_op jit(solution)/shard_map/ppermute | solution.py:234
  160.2 11.5 %gate_wgrad.1 = bf16[4096,1792]{1,0:T(8,128)(2,1)} custom-call(bf16[256,4096]{1,0:T(8,128)(2,1)S(1)} %copy-done.4, bf16[256,4096]{1,0:T(8,128)(2,1)S(1)} %copy-done.3, bf16[256,1792]{1,0:T(8,128)(2,1)S(1)} %copy-done.11, bf16[256,1792]{1,0:T(8,128)(2,1)S(1)} %copy-done.8), custom_call_target="tpu_custom_call" | custom-call | flops 7516192768 | bytes 14680064 | tf_op jit(solution)/shard_map/gate_wgrad/pallas_call | solution.py:199
  172.0 1.8 collective-permute-start.23
  173.8 11.5 %up_wgrad.1 = bf16[4096,1792]{1,0:T(8,128)(2,1)} custom-call(bf16[256,4096]{1,0:T(8,128)(2,1)S(1)} %copy-done.4, bf16[256,4096]{1,0:T(8,128)(2,1)S(1)} %copy-done.3, bf16[256,1792]{1,0:T(8,128)(2,1)S(1)} %copy-done.9, bf16[256,1792]{1,0:T(8,128)(2,1)S(1)} %copy-done.7), custom_call_target="tpu_custom_call" | custom-call | flops 7516192768 | bytes 14680064 | tf_op jit(solution)/shard_map/up_wgrad/pallas_call | solution.py:199
  (72 shorter events, 8.8 us)
Async XLA Ops:
  0.6 18.1 %collective-permute-start = (bf16[64,4096]{1,0:T(8,128)(2,1)}, bf16[64,4096]{1,0:T(8,128)(2,1)S(1)}, u32[]{:S(2)}, u32[]{:S(2)}) collective-permute-start(bf16[64,4096]{1,0:T(8,128)(2,1)} %refs_2_), channel_id=1, source_target_pairs={{0,4},{2,6},{4,8},{6,10},{8,12},{10,14},{12,0},{14,2},{1,5},{3,7},... | collective-permute-start | bytes 1572872 | tf_op jit(solution)/shard_map/ppermute | solution.py:234
  3.7 15.1 %collective-permute-start.1 = (bf16[64,4096]{1,0:T(8,128)(2,1)}, bf16[64,4096]{1,0:T(8,128)(2,1)S(1)}, u32[]{:S(2)}, u32[]{:S(2)}) collective-permute-start(bf16[64,4096]{1,0:T(8,128)(2,1)} %refs_2_), channel_id=1, source_target_pairs={{0,2},{2,0},{4,6},{6,4},{8,10},{10,8},{12,14},{14,12},{1,3},{3,1},... | collective-permute-start | bytes 1572872 | tf_op jit(solution)/shard_map/ppermute | solution.py:237
  5.2 24.7 %collective-permute-start.4 = (bf16[64,4096]{1,0:T(8,128)(2,1)}, bf16[64,4096]{1,0:T(8,128)(2,1)S(1)}, u32[]{:S(2)}, u32[]{:S(2)}) collective-permute-start(bf16[64,4096]{1,0:T(8,128)(2,1)} %refs_2_), channel_id=1, source_target_pairs={{0,12},{2,14},{4,0},{6,2},{8,4},{10,6},{12,8},{14,10},{1,13},{3,15... | collective-permute-start | bytes 1572872 | tf_op jit(solution)/shard_map/ppermute | solution.py:234
  7.5 22.6 %collective-permute-start.5 = (bf16[64,4096]{1,0:T(8,128)(2,1)}, bf16[64,4096]{1,0:T(8,128)(2,1)}, u32[]{:S(2)}, u32[]{:S(2)}) collective-permute-start(bf16[64,4096]{1,0:T(8,128)(2,1)} %refs_2_.1), channel_id=1, source_target_pairs={{0,2},{2,0},{4,6},{6,4},{8,10},{10,8},{12,14},{14,12},{1,3},{3,1},... | collective-permute-start | bytes 1572872 | tf_op jit(solution)/shard_map/ppermute | solution.py:237
  13.0 27.4 %copy-start.2 = (bf16[64,4096]{1,0:T(8,128)(2,1)S(1)}, bf16[64,4096]{1,0:T(8,128)(2,1)}, u32[]{:S(2)}) copy-start(bf16[64,4096]{1,0:T(8,128)(2,1)} %refs_2_.1) | copy-start | bytes 1572868
  18.8 21.6 %collective-permute-start.2 = (bf16[64,4096]{1,0:T(8,128)(2,1)S(1)}, bf16[64,4096]{1,0:T(8,128)(2,1)S(1)}, u32[]{:S(2)}, u32[]{:S(2)}) collective-permute-start(bf16[64,4096]{1,0:T(8,128)(2,1)S(1)} %collective-permute-done.refs_0_), channel_id=1, source_target_pairs={{0,4},{2,6},{4,8},{6,10},{8,12},{10,14},{12,0},{14,2},{1,5},{3,7},... | collective-permute-start | bytes 1572872 | tf_op jit(solution)/shard_map/ppermute | solution.py:234
  20.3 20.0 %collective-permute-start.3 = (bf16[64,4096]{1,0:T(8,128)(2,1)S(1)}, bf16[64,4096]{1,0:T(8,128)(2,1)S(1)}, u32[]{:S(2)}, u32[]{:S(2)}) collective-permute-start(bf16[64,4096]{1,0:T(8,128)(2,1)S(1)} %collective-permute-done.refs_0_), channel_id=1, source_target_pairs={{0,2},{2,0},{4,6},{6,4},{8,10},{10,8},{12,14},{14,12},{1,3},{3,1},... | collective-permute-start | bytes 1572872 | tf_op jit(solution)/shard_map/ppermute | solution.py:237
  27.1 44.5 %copy-start = (bf16[4096,1792]{1,0:T(8,128)(2,1)}, bf16[4096,1792]{1,0:T(8,128)(2,1)S(1)}, u32[]{:S(2)}) copy-start(bf16[4096,1792]{1,0:T(8,128)(2,1)S(1)} %hold_up.1.refs_5_) | copy-start | bytes 44040196
  27.1 31.7 %copy-start.1 = (bf16[64,4096]{1,0:T(8,128)(2,1)S(1)}, bf16[64,4096]{1,0:T(8,128)(2,1)}, u32[]{:S(2)}) copy-start(bf16[64,4096]{1,0:T(8,128)(2,1)} %refs_2_) | copy-start | bytes 1572868
  40.4 16.9 %collective-permute-start.7 = (bf16[64,4096]{1,0:T(8,128)(2,1)S(1)}, bf16[64,4096]{1,0:T(8,128)(2,1)}, u32[]{:S(2)}, u32[]{:S(2)}) collective-permute-start(bf16[64,4096]{1,0:T(8,128)(2,1)S(1)} %copy-done.2), channel_id=1, source_target_pairs={{0,12},{2,14},{4,0},{6,2},{8,4},{10,6},{12,8},{14,10},{1,13},{3,15... | collective-permute-start | bytes 1572872 | tf_op jit(solution)/shard_map/ppermute | solution.py:234
  42.2 26.8 %collective-permute-start.9 = (bf16[64,4096]{1,0:T(8,128)(2,1)S(1)}, bf16[64,4096]{1,0:T(8,128)(2,1)}, u32[]{:S(2)}, u32[]{:S(2)}) collective-permute-start(bf16[64,4096]{1,0:T(8,128)(2,1)S(1)} %copy-done.2), channel_id=1, source_target_pairs={{0,4},{2,6},{4,8},{6,10},{8,12},{10,14},{12,0},{14,2},{1,5},{3,7},... | collective-permute-start | bytes 1572872 | tf_op jit(solution)/shard_map/ppermute | solution.py:234
  42.4 14.9 %collective-permute-start.6 = (bf16[64,4096]{1,0:T(8,128)(2,1)S(1)}, bf16[64,4096]{1,0:T(8,128)(2,1)S(1)}, u32[]{:S(2)}, u32[]{:S(2)}) collective-permute-start(bf16[64,4096]{1,0:T(8,128)(2,1)S(1)} %collective-permute-done.4.refs_0_), channel_id=1, source_target_pairs={{0,2},{2,0},{4,6},{6,4},{8,10},{10,8},{12,14},{14,12},{1,3},{3,1},... | collective-permute-start | bytes 1572872 | tf_op jit(solution)/shard_map/ppermute | solution.py:237
  43.9 25.0 %collective-permute-start.8 = (bf16[64,4096]{1,0:T(8,128)(2,1)S(1)}, bf16[64,4096]{1,0:T(8,128)(2,1)S(1)}, u32[]{:S(2)}, u32[]{:S(2)}) collective-permute-start(bf16[64,4096]{1,0:T(8,128)(2,1)S(1)} %collective-permute-done.2.refs_2_), channel_id=1, source_target_pairs={{0,2},{2,0},{4,6},{6,4},{8,10},{10,8},{12,14},{14,12},{1,3},{3,1},... | collective-permute-start | bytes 1572872 | tf_op jit(solution)/shard_map/ppermute | solution.py:237
  57.3 24.4 %collective-permute-start.10 = (bf16[64,4096]{1,0:T(8,128)(2,1)}, bf16[64,4096]{1,0:T(8,128)(2,1)}, u32[]{:S(2)}, u32[]{:S(2)}) collective-permute-start(bf16[64,4096]{1,0:T(8,128)(2,1)} %collective-permute-done.7.refs_0_), channel_id=1, source_target_pairs={{0,2},{2,0},{4,6},{6,4},{8,10},{10,8},{12,14},{14,12},{1,3},{3,1},... | collective-permute-start | bytes 1572872 | tf_op jit(solution)/shard_map/ppermute | solution.py:237
  69.0 14.3 %collective-permute-start.11 = (bf16[64,4096]{1,0:T(8,128)(2,1)}, bf16[64,4096]{1,0:T(8,128)(2,1)S(1)}, u32[]{:S(2)}, u32[]{:S(2)}) collective-permute-start(bf16[64,4096]{1,0:T(8,128)(2,1)} %collective-permute-done.9.refs_0_), channel_id=1, source_target_pairs={{0,4},{2,6},{4,8},{6,10},{8,12},{10,14},{12,0},{14,2},{1,5},{3,7},... | collective-permute-start | bytes 1572872 | tf_op jit(solution)/shard_map/ppermute | solution.py:234
  70.0 22.2 %collective-permute-start.13 = (bf16[64,4096]{1,0:T(8,128)(2,1)}, bf16[64,4096]{1,0:T(8,128)(2,1)S(1)}, u32[]{:S(2)}, u32[]{:S(2)}) collective-permute-start(bf16[64,4096]{1,0:T(8,128)(2,1)} %collective-permute-done.5.refs_3_), channel_id=1, source_target_pairs={{0,4},{2,6},{4,8},{6,10},{8,12},{10,14},{12,0},{14,2},{1,5},{3,7},... | collective-permute-start | bytes 1572872 | tf_op jit(solution)/shard_map/ppermute | solution.py:234
  83.3 9.2 %collective-permute-start.12 = (bf16[64,4096]{1,0:T(8,128)(2,1)S(1)}, bf16[64,4096]{1,0:T(8,128)(2,1)S(1)}, u32[]{:S(2)}, u32[]{:S(2)}) collective-permute-start(bf16[64,4096]{1,0:T(8,128)(2,1)S(1)} %collective-permute-done.11.refs_2_), channel_id=1, source_target_pairs={{0,2},{2,0},{4,6},{6,4},{8,10},{10,8},{12,14},{14,12},{1,3},{3,1},... | collective-permute-start | bytes 1572872 | tf_op jit(solution)/shard_map/ppermute | solution.py:237
  92.5 8.4 %collective-permute-start.14 = (bf16[2,256,1792]{2,1,0:T(8,128)(2,1)S(1)}, bf16[2,256,1792]{2,1,0:T(8,128)(2,1)S(1)}, u32[]{:S(2)}, u32[]{:S(2)}) collective-permute-start(bf16[2,256,1792]{2,1,0:T(8,128)(2,1)S(1)} %copy-done.18), channel_id=1, source_target_pairs={{0,1},{1,0},{2,3},{3,2},{4,5},{5,4},{6,7},{7,6},{8,9},{9,8},{10,11... | collective-permute-start | bytes 5505032 | tf_op jit(solution)/shard_map/ppermute | solution.py:240
  92.5 29.5 %collective-permute-start.18 = (bf16[2,256,1792]{2,1,0:T(8,128)(2,1)S(1)}, bf16[2,256,1792]{2,1,0:T(8,128)(2,1)S(1)}, u32[]{:S(2)}, u32[]{:S(2)}) collective-permute-start(bf16[2,256,1792]{2,1,0:T(8,128)(2,1)S(1)} %copy-done.17), channel_id=1, source_target_pairs={{0,1},{1,0},{2,3},{3,2},{4,5},{5,4},{6,7},{7,6},{8,9},{9,8},{10,11... | collective-permute-start | bytes 5505032 | tf_op jit(solution)/shard_map/ppermute | solution.py:240
  93.0 7.9 %collective-permute-start.15 = (bf16[1,256,1792]{2,1,0:T(8,128)(2,1)}, bf16[1,256,1792]{2,1,0:T(8,128)(2,1)S(1)}, u32[]{:S(2)}, u32[]{:S(2)}) collective-permute-start(bf16[1,256,1792]{2,1,0:T(8,128)(2,1)} %get-tuple-element.224), channel_id=1, source_target_pairs={{0,1},{1,0},{2,3},{3,2},{4,5},{5,4},{6,7},{7,6},{8,9},{9,8},{10,11... | collective-permute-start | bytes 2752520 | tf_op jit(solution)/shard_map/ppermute | solution.py:240
  100.3 21.6 %collective-permute-start.19 = (bf16[1,256,1792]{2,1,0:T(8,128)(2,1)}, bf16[1,256,1792]{2,1,0:T(8,128)(2,1)S(1)}, u32[]{:S(2)}, u32[]{:S(2)}) collective-permute-start(bf16[1,256,1792]{2,1,0:T(8,128)(2,1)} %get-tuple-element.247), channel_id=1, source_target_pairs={{0,1},{1,0},{2,3},{3,2},{4,5},{5,4},{6,7},{7,6},{8,9},{9,8},{10,11... | collective-permute-start | bytes 2752520 | tf_op jit(solution)/shard_map/ppermute | solution.py:240
  119.8 21.0 %copy-start.14 = (bf16[64,4096]{1,0:T(8,128)(2,1)S(1)}, bf16[64,4096]{1,0:T(8,128)(2,1)}, u32[]{:S(2)}) copy-start(bf16[64,4096]{1,0:T(8,128)(2,1)} %get-tuple-element.274) | copy-start | bytes 1572868
  119.8 24.0 %copy-start.5 = (bf16[256,4096]{1,0:T(8,128)(2,1)S(1)}, bf16[256,4096]{1,0:T(8,128)(2,1)}, u32[]{:S(2)}) copy-start(bf16[256,4096]{1,0:T(8,128)(2,1)} %get-tuple-element.261.refs_3_) | copy-start | bytes 6291460
  119.8 24.0 %copy-start.6 = (bf16[256,4096]{1,0:T(8,128)(2,1)S(1)}, bf16[256,4096]{1,0:T(8,128)(2,1)}, u32[]{:S(2)}) copy-start(bf16[256,4096]{1,0:T(8,128)(2,1)} %get-tuple-element.260.refs_2_) | copy-start | bytes 6291460
  119.8 24.0 %copy-start.10 = (bf16[256,1792]{1,0:T(8,128)(2,1)S(1)}, bf16[256,1792]{1,0:T(8,128)(2,1)}, u32[]{:S(2)}) copy-start(bf16[256,1792]{1,0:T(8,128)(2,1)} %get-tuple-element.259.refs_1_) | copy-start | bytes 2752516
  119.9 21.0 %collective-permute-start.17 = (bf16[64,4096]{1,0:T(8,128)(2,1)}, bf16[64,4096]{1,0:T(8,128)(2,1)S(1)}, u32[]{:S(2)}, u32[]{:S(2)}) collective-permute-start(bf16[64,4096]{1,0:T(8,128)(2,1)} %get-tuple-element.244), channel_id=1, source_target_pairs={{0,2},{2,0},{4,6},{6,4},{8,10},{10,8},{12,14},{14,12},{1,3},{3,1},... | collective-permute-start | bytes 1572872 | tf_op jit(solution)/shard_map/ppermute | solution.py:237
  121.2 64.1 %collective-permute-start.16 = (bf16[64,4096]{1,0:T(8,128)(2,1)}, bf16[64,4096]{1,0:T(8,128)(2,1)S(1)}, u32[]{:S(2)}, u32[]{:S(2)}) collective-permute-start(bf16[64,4096]{1,0:T(8,128)(2,1)} %get-tuple-element.243), channel_id=1, source_target_pairs={{0,2},{2,0},{4,6},{6,4},{8,10},{10,8},{12,14},{14,12},{1,3},{3,1},... | collective-permute-start | bytes 1572872 | tf_op jit(solution)/shard_map/ppermute | solution.py:237
  141.0 44.3 %collective-permute-start.24 = (bf16[64,4096]{1,0:T(8,128)(2,1)S(1)}, bf16[64,4096]{1,0:T(8,128)(2,1)S(1)}, u32[]{:S(2)}, u32[]{:S(2)}) collective-permute-start(bf16[64,4096]{1,0:T(8,128)(2,1)S(1)} %add_convert_fusion.1), channel_id=1, source_target_pairs={{0,4},{2,6},{4,8},{6,10},{8,12},{10,14},{12,0},{14,2},{1,5},{3,7},... | collective-permute-start | bytes 1572872 | tf_op jit(solution)/shard_map/ppermute | solution.py:234
  141.8 15.6 %collective-permute-start.20 = (bf16[64,4096]{1,0:T(8,128)(2,1)}, bf16[64,4096]{1,0:T(8,128)(2,1)S(1)}, u32[]{:S(2)}, u32[]{:S(2)}) collective-permute-start(bf16[64,4096]{1,0:T(8,128)(2,1)} %get-tuple-element.257), channel_id=1, source_target_pairs={{0,2},{2,0},{4,6},{6,4},{8,10},{10,8},{12,14},{14,12},{1,3},{3,1},... | collective-permute-start | bytes 1572872 | tf_op jit(solution)/shard_map/ppermute | solution.py:237
  142.8 29.0 %collective-permute-start.22 = (bf16[64,4096]{1,0:T(8,128)(2,1)}, bf16[64,4096]{1,0:T(8,128)(2,1)S(1)}, u32[]{:S(2)}, u32[]{:S(2)}) collective-permute-start(bf16[64,4096]{1,0:T(8,128)(2,1)} %get-tuple-element.265), channel_id=1, source_target_pairs={{0,2},{2,0},{4,6},{6,4},{8,10},{10,8},{12,14},{14,12},{1,3},{3,1},... | collective-permute-start | bytes 1572872 | tf_op jit(solution)/shard_map/ppermute | solution.py:237
  157.5 14.2 %collective-permute-start.21 = (bf16[64,4096]{1,0:T(8,128)(2,1)S(1)}, bf16[64,4096]{1,0:T(8,128)(2,1)S(1)}, u32[]{:S(2)}, u32[]{:S(2)}) collective-permute-start(bf16[64,4096]{1,0:T(8,128)(2,1)S(1)} %add_convert_fusion.3), channel_id=1, source_target_pairs={{0,12},{2,14},{4,0},{6,2},{8,4},{10,6},{12,8},{14,10},{1,13},{3,15... | collective-permute-start | bytes 1572872 | tf_op jit(solution)/shard_map/ppermute | solution.py:234
  172.0 13.4 %collective-permute-start.23 = (bf16[64,4096]{1,0:T(8,128)(2,1)S(1)}, bf16[64,4096]{1,0:T(8,128)(2,1)S(1)}, u32[]{:S(2)}, u32[]{:S(2)}) collective-permute-start(bf16[64,4096]{1,0:T(8,128)(2,1)S(1)} %add_convert_fusion.2), channel_id=1, source_target_pairs={{0,12},{2,14},{4,0},{6,2},{8,4},{10,6},{12,8},{14,10},{1,13},{3,15... | collective-permute-start | bytes 1572872 | tf_op jit(solution)/shard_map/ppermute | solution.py:234
  (12 other events, 173.1 us)
